TPU v7x, 32 devices: a whole 2x2x4 slice. The times are simulated.
32 devices in a mesh: member: 2 (over x), band: 16 (over z, y, core).
Axes of the slice: x: 2, y: 2, z: 4, core: 2. Of those that a mesh axis runs over, the one named last changes fastest.
Arguments:
- state: float32 [14, 6, 2048, 1024], P('member', None, 'band'), parts along dimension 0, may hold values from -6 to 6
- courant_lon: float32 [4096, 1024], P(('member', 'band')), parts along dimension 0, may hold values from 0.05 to 0.45
- courant_lat: float32 [4096, 1024], P(('member', 'band')), parts along dimension 0, may hold values from 0.05 to 0.45
- reference_field: float32 [12, 2048, 1024], P('member', 'band'), parts along dimension 0, may hold values from -6 to 6
- nudge_rate: float32 [512], replicated, may hold values from 0.05 to 1
Outputs:
- new_state: float32 [14, 6, 2048, 1024], P('member', None, 'band'), parts along dimension 0
There are 2 independent parts, one for each index of `member`. A program takes and returns all parts, laid end to end along the dimension named above; an argument that names none is the same for every part. Nothing has to cross between parts.
All inputs are finite; a program needn't handle non-finite values.
Results may differ from a plain program's by a relative error of at most 0.0003.
Values sent between devices are 32-bit elements; how exact they have to be, the bound alone decides.
A program may use at most 256 MiB of HBM per device.

v0:
```python
import math

import jax
import jax.numpy as jnp
from jax import lax
from jax.sharding import PartitionSpec as P

STEPS = 2


highest = lax.Precision.HIGHEST


def passed_along(value, axis, by):
    peers = lax.axis_size(axis)
    return lax.ppermute(value, axis, [(i, (i + by) % peers) for i in range(peers)])


def latitude_terms(lat_total):
    centres = (jnp.arange(lat_total).astype(jnp.float32) + 0.5) * (math.pi / lat_total)
    return (jnp.cos(centres), jnp.log(jnp.sin(centres)), jnp.sin(centres) * (math.pi / lat_total))


def norm_table(wave_total):
    orders = jnp.arange(1, wave_total).astype(jnp.float32)
    terms = jnp.log((2.0 * orders + 1.0) / (2.0 * orders))
    return jnp.concatenate([jnp.zeros((1,), jnp.float32), jnp.cumsum(terms)])


def start_value(wave_ids, log_sin, norms):
    matches = wave_ids[:, None] == jnp.arange(norms.shape[0])[None, :]
    log_norm = jnp.sum(jnp.where(matches, norms[None, :], 0.0), axis=1)
    orders = wave_ids.astype(jnp.float32)
    return 0.5 * log_norm[:, None] + orders[:, None] * log_sin[None, :] - 0.5 * math.log(2.0)


def legendre_table(wave_rows, offset_rows, upper_rows, starts, cosines):

    def advance(carry, inputs):
        earlier, latest, deficit = carry
        wave_now, offset_now, upper_now = inputs
        orders = wave_now.astype(jnp.float32)[:, None]
        degree = (wave_now + offset_now).astype(jnp.float32)[:, None]
        factor_now = jnp.sqrt(
            (4.0 * degree * degree - 1.0) / jnp.maximum(degree * degree - orders * orders, 1.0)
        )
        below = degree - 1.0
        older_sq = jnp.where(
            offset_now[:, None] >= 2,
            (4.0 * below * below - 1.0) / jnp.maximum(below * below - orders * orders, 1.0),
            1.0,
        )
        factor_old = jnp.where(offset_now[:, None] >= 2, factor_now / jnp.sqrt(older_sq), 0.0)
        log_start = jnp.where(upper_now[:, None] == 1, starts[:, 1], starts[:, 0])
        clamped = jnp.maximum(log_start, -80.0)
        fresh = offset_now[:, None] == 0
        recurred = factor_now * cosines[None, :] * latest - factor_old * earlier
        largest = jnp.maximum(jnp.abs(recurred), jnp.abs(latest))
        absorb = jnp.maximum(deficit, -jnp.log(jnp.maximum(largest, 1.0)))
        rescale = jnp.exp(absorb)
        next_latest = jnp.where(fresh, jnp.exp(clamped), recurred * rescale)
        next_earlier = jnp.where(fresh, jnp.zeros_like(latest), latest * rescale)
        next_deficit = jnp.where(fresh, log_start - clamped, deficit - absorb)
        result_row = next_latest * jnp.exp(next_deficit)
        return ((next_earlier, next_latest, next_deficit), result_row)

    zero_row = jnp.zeros_like(starts[:, 0])
    final_carry, rows = lax.scan(
        advance,
        (zero_row, zero_row, zero_row),
        (wave_rows.T, offset_rows.T, upper_rows.T),
        unroll=16,
    )
    return jnp.transpose(rows, (1, 0, 2))


def rate_lookup(degrees, rate_table):
    matches = degrees[..., None] == jnp.arange(rate_table.shape[0])
    return jnp.sum(jnp.where(matches, rate_table, 0.0), axis=-1)


def advect(cells, west_edge, lon_courant, lat_courant):
    west_cells = jnp.concatenate([west_edge, cells[:, :, :-1]], axis=2)
    south_cells = jnp.concatenate([jnp.zeros_like(cells[:, :, :, :1]), cells[:, :, :, :-1]], axis=3)
    return cells - lon_courant * (cells - west_cells) - lat_courant * (cells - south_cells)


def body(state, courant_lon, courant_lat, reference_field, nudge_rate):
    level_count = state.shape[1]
    lon_local = state.shape[2]
    lat_total = state.shape[3]
    band_count = lax.axis_size("band")
    band_place = lax.axis_index("band")
    lon_total = lon_local * band_count
    wave_total = nudge_rate.shape[0]
    wave_local = wave_total // band_count
    advected = state
    for turn_index in range(STEPS):
        west_column = passed_along(advected[:, :, -1:], "band", 1)
        advected = advect(advected, west_column, courant_lon, courant_lat)
    anomaly = reference_field - advected[0]
    lon_iota = jnp.arange(lon_total)
    wave_iota = jnp.arange(wave_total)
    phase = (lon_iota[:, None] * wave_iota[None, :] % lon_total).astype(jnp.float32) * (
        2.0 * math.pi / lon_total
    )
    cos_table = jnp.cos(phase)
    sin_table = jnp.sin(phase)
    forward = jnp.concatenate([cos_table, -sin_table], axis=1) / lon_total
    doubling = jnp.where(wave_iota == 0, 1.0, 2.0)[:, None]
    inverse = jnp.concatenate([cos_table.T * doubling, -sin_table.T * doubling], axis=0)
    fourier = jnp.einsum(
        "lij,ik->klj",
        lax.all_to_all(anomaly, "band", split_axis=2, concat_axis=1, tiled=True),
        forward,
        precision=highest,
    )
    spectrum = fourier.reshape(2, wave_total, level_count, fourier.shape[2])
    lat_local = spectrum.shape[3]
    cosines, log_sin, quad_weights = latitude_terms(lat_total)
    norms = norm_table(wave_total)
    wave_ids = band_place * wave_local + jnp.arange(wave_local)
    wave_rows = jnp.broadcast_to(wave_ids[:, None], (wave_local, wave_total))
    offset_rows = jnp.broadcast_to(jnp.arange(wave_total)[None, :], (wave_local, wave_total))
    initial = start_value(wave_ids, log_sin, norms)
    legendre = legendre_table(
        wave_rows, offset_rows, jnp.zeros_like(wave_rows), jnp.stack([initial, initial], 1), cosines
    )
    rate_rows = rate_lookup(wave_rows + offset_rows, nudge_rate)
    weighted = (
        lax.all_to_all(spectrum, "band", split_axis=1, concat_axis=3, tiled=True) * quad_weights
    )
    analysed = jnp.einsum("skj,cslj->skcl", legendre, weighted, precision=highest)
    scaled = analysed * rate_rows[:, :, None, None]
    waves_out = jnp.einsum("skj,skcl->cslj", legendre, scaled, precision=highest)
    gathered = lax.all_to_all(waves_out, "band", split_axis=3, concat_axis=1, tiled=True)
    level_part = gathered.shape[2]
    flattened = gathered.reshape(2 * wave_total, level_part, lat_local)
    band_increment = jnp.einsum("klj,ki->lij", flattened, inverse, precision=highest)
    increment = lax.all_to_all(band_increment, "band", split_axis=1, concat_axis=2, tiled=True)
    nudged = advected[0] + increment
    return jnp.concatenate([nudged[None], advected[1:]], axis=0)


def solution(mesh):
    placed = (
        P("member", None, "band", None),
        P(("member", "band"), None),
        P(("member", "band"), None),
        P("member", "band", None),
        P(),
    )
    return jax.shard_map(
        body, mesh=mesh, in_specs=placed, out_specs=P("member", None, "band", None), check_vma=False
    )
```

profile of v0, /device:TPU:15, one launch (start us, length us, event | category | flops | bytes accessed | tf_op | source)
XLA Modules:
  0.0 927.3 jit_solution(11728541990109933526)
XLA Ops:
  0.0 1.5 slice.307
  1.5 1.9 collective-permute-start
  3.4 21.6 %copy.111 = f32[7,6,128,1024]{2,3,1,0:T(8,128)} copy(f32[7,6,128,1024]{3,2,1,0:T(8,128)} %param.7) | data formatting | bytes 44040192 | tf_op args[0]
  25.4 10.5 %copy.109 = f32[7,6,1,1024]{2,3,1,0:T(8,128)} copy(f32[7,6,1,1024]{3,2,1,0:T(1,128)S(1)} %collective-permute-done) | data formatting | bytes 344064 | tf_op jit(solution)/shard_map/ppermute | solution.py:16
  35.9 36.4 %fusion.157 = f32[7,6,128,1024]{2,3,1,0:T(8,128)} fusion(f32[7,6,128,1024]{2,3,1,0:T(8,128)} %copy.111, f32[7,6,127,1024]{2,3,1,0:T(8,128)} %bitcast.695, f32[7,6,1,1024]{2,3,1,0:T(8,128)} %copy.109, f32[7,6,128,1023]{2,3,1,0:T(8,128)} %bitcast.696, f32[128,1024]{0,1:T(8,128)S(1)} %copy.112, f32[128,1024]{0,1:T(8,128)S(1)} %copy.107), kind=kLoop, calls=%fused_computation.404 | loop fusion | flops 38535168 | bytes 89107456 | tf_op jit(solution)/shard_map/sub | solution.py:85
  72.3 18.3 %slice.384 = f32[7,6,1,1024]{2,3,1,0:T(8,128)} slice(f32[7,6,128,1024]{2,3,1,0:T(8,128)} %fusion.157), slice={[0:7], [0:6], [127:128], [0:1024]} | slice | bytes 344064 | tf_op jit(solution)/shard_map/slice | solution.py:99
  90.5 11.8 %copy.115 = f32[7,6,1,1024]{3,2,1,0:T(1,128)S(1)} copy(f32[7,6,1,1024]{2,3,1,0:T(8,128)} %slice.384) | data formatting | bytes 344064 | tf_op jit(solution)/shard_map/slice | solution.py:99
  102.5 2.4 copy.118
  104.8 10.5 %copy.116 = f32[7,6,1,1024]{2,3,1,0:T(8,128)} copy(f32[7,6,1,1024]{3,2,1,0:T(1,128)S(1)} %collective-permute-done.1) | data formatting | bytes 344064 | tf_op jit(solution)/shard_map/ppermute | solution.py:16
  115.3 37.1 %fusion.160 = f32[7,6,128,1024]{2,3,1,0:T(8,128)} fusion(f32[7,6,128,1024]{2,3,1,0:T(8,128)} %fusion.157, f32[7,6,127,1024]{2,3,1,0:T(8,128)} %bitcast.693, f32[7,6,1,1024]{2,3,1,0:T(8,128)} %copy.116, f32[7,6,128,1023]{2,3,1,0:T(8,128)} %bitcast.694, f32[128,1024]{0,1:T(8,128)} %copy-done.1, f32[128,1024]{0,1:T(8,128)} %copy-done), kind=kLoop, calls=%fused_computation.408 | loop fusion | flops 38535168 | bytes 89107456 | tf_op jit(solution)/shard_map/sub | solution.py:85
  152.4 2.2 bitcast_subtract_fusion.32
  154.6 3.9 copy.119
  158.5 9.0 all-to-all-start
  169.1 16.4 %sine_negate_fusion = (f32[2048,512]{0,1:T(8,128)S(1)}, f32[2048,512]{0,1:T(8,128)S(1)}) fusion(), kind=kLoop, calls=%fused_computation.427 | loop fusion | flops 15728640 | bytes 8388608 | tf_op jit(solution)/shard_map/neg | solution.py:109
  185.6 4.1 maximum_multiply_fusion
  189.7 70.2 %all-to-all-done = f32[6,128,1024]{1,0,2:T(8,128)} async-done(((f32[6,128,1024]{1,0,2:T(8,128)}), f32[6,128,1024]{1,0,2:T(8,128)}, u32[]{:S(2)}, u32[]{:S(2)}) %all-to-all-start) | async-done | bytes 3145760 | tf_op jit(solution)/shard_map/all_to_all | solution.py:114
  259.8 4.0 copy.121
  263.9 2.5 reshape.1941
  266.4 14.5 %fusion.241 = f32[2,512,6,64]{1,3,2,0:T(8,128)} fusion(f32[2,512,2048,1]{2,1,3,0:T(8,128)} %bitcast.697, f32[6,2048,64,1]{1,2,0,3:T(8,128)} %reshape.1941), kind=kOutput, calls=%fused_computation.462 | convolution fusion | flops 9663676416 | bytes 13107200 | tf_op jit(solution)/shard_map/lij,ik->klj/dot_general | solution.py:112
  280.9 4.2 copy.122
  285.1 4.2 reshape.1947
  289.4 5.2 all-to-all-start.1
  295.4 173.3 %while.21 = (s32[]{:T(128)}, f32[32,1024]{1,0:T(8,128)S(1)}, f32[32,1024]{1,0:T(8,128)S(1)}, f32[32,1024]{1,0:T(8,128)S(1)}, f32[32,16,32,1024]{3,2,1,0:T(8,128)...) while((s32[]{:T(128)}, f32[32,1024]{1,0:T(8,128)S(1)}, ...), condition=%wide.region_4.5_spmd.clone.clone, body=%wide.region_3.4_spmd.clone.clone.sunk | while | flops 15023121 | bytes 23396332 | solution.py:68
  310.1 1.5 bitcast_dynamic-update-slice_fusion.50
  315.5 1.5 bitcast_dynamic-update-slice_fusion.50
  320.9 1.5 bitcast_dynamic-update-slice_fusion.50
  358.8 1.5 bitcast_dynamic-update-slice_fusion.50
  364.3 1.5 bitcast_dynamic-update-slice_fusion.50
  375.1 1.5 bitcast_dynamic-update-slice_fusion.50
  391.3 1.5 bitcast_dynamic-update-slice_fusion.50
  407.6 1.5 bitcast_dynamic-update-slice_fusion.50
  418.4 1.5 bitcast_dynamic-update-slice_fusion.50
  434.6 1.5 bitcast_dynamic-update-slice_fusion.50
  450.9 1.5 bitcast_dynamic-update-slice_fusion.50
  461.7 1.5 bitcast_dynamic-update-slice_fusion.50
  468.8 6.4 select_reduce_fusion
  475.8 6.1 reduce.2
  482.0 3.4 reshape.1948
  485.7 2.2 copy.124
  487.9 1.8 all_to_all.57
  489.7 1.6 broadcast_multiply_fusion
  491.3 107.1 %fusion.182 = f32[32,512,2,6]{1,3,2,0:T(8,128)S(1)} fusion(f32[2,32,6,1024]{3,1,2,0:T(8,128)S(1)} %broadcast_multiply_fusion, f32[512,32,1024]{2,1,0:T(8,128)} %bitcast.2, f32[32,512]{1,0:T(8,128)S(1)} %select_reduce_fusion), kind=kOutput, calls=%fused_computation.441 | convolution fusion | flops 2416115712 | bytes 69533696 | tf_op jit(solution)/shard_map/skj,cslj->skcl/dot_general | solution.py:133
  598.4 85.2 %fusion.179 = f32[2,32,6,1024]{3,2,0,1:T(8,128)S(1)} fusion(f32[32,512,2,6]{1,3,2,0:T(8,128)S(1)} %fusion.182, f32[512,32,1024]{2,1,0:T(8,128)} %bitcast.2), kind=kOutput, calls=%fused_computation.440 | convolution fusion | flops 2415919104 | bytes 69468160 | tf_op jit(solution)/shard_map/skj,skcl->cslj/dot_general | solution.py:135
  683.7 5.2 copy.126
  688.8 8.8 reshape.1949
  697.6 6.0 all-to-all-start.2
  703.7 18.1 %cosine_multiply_fusion = (f32[512,2048]{1,0:T(8,128)}, f32[512,2048]{1,0:T(8,128)}) fusion(f32[512]{0:T(512)S(1)} %fusion.190), kind=kLoop, calls=%fused_computation.431 | loop fusion | flops 17825792 | bytes 8390656 | tf_op jit(solution)/shard_map/mul | solution.py:111
  721.7 18.1 %all-to-all-done.2 = f32[16,1,24576]{2,1,0:T(1,128)S(1)} async-done(((f32[16,1,24576]{2,1,0:T(1,128)}), f32[16,1,24576]{2,1,0:T(1,128)S(1)}, u32[]{:S(2)}, u32[]{:S(2)}) %all-to-all-start.2) | async-done | bytes 1572896 | tf_op jit(solution)/shard_map/all_to_all | solution.py:136
  739.8 4.4 reduce.3
  744.2 7.0 reshape.1950
  751.2 7.8 copy.138
  759.0 2.1 copy.129
  761.1 13.1 %fusion.161 = f32[2048,384]{0,1:S(1)} fusion(f32[1024,384]{0,1:T(8,128)} %bitcast.707, f32[512,2048]{1,0:T(8,128)} %get-tuple-element.510, f32[512,2048]{1,0:T(8,128)} %get-tuple-element.509), kind=kOutput, calls=%fused_computation.410 | convolution fusion | flops 9665773568 | bytes 13107200
  774.2 4.8 copy.130
  779.0 12.5 %reshape.1951 = f32[16,1,49152]{2,1,0:T(1,128)} reshape(f32[2048,6,64]{2,1,0:T(8,128)} %bitcast.698) | data formatting | bytes 6291456
  791.5 5.2 all-to-all-start.3
  796.7 14.4 %slice.388 = f32[6,6,128,1024]{2,3,1,0:T(8,128)} slice(f32[7,6,128,1024]{2,3,1,0:T(8,128)} %fusion.160), slice={[1:7], [0:6], [0:128], [0:1024]} | slice | bytes 37748736 | tf_op jit(solution)/shard_map/slice | solution.py:142
  811.0 55.4 %all-to-all-done.3 = f32[16,1,49152]{2,1,0:T(1,128)S(1)} async-done(((f32[16,1,49152]{2,1,0:T(1,128)}), f32[16,1,49152]{2,1,0:T(1,128)S(1)}, u32[]{:S(2)}, u32[]{:S(2)}) %all-to-all-start.3) | async-done | bytes 3145760 | tf_op jit(solution)/shard_map/all_to_all | solution.py:140
  866.5 10.8 %reduce.4 = f32[16,49152]{1,0:T(8,128)} reduce(f32[16,1,49152]{2,1,0:T(1,128)S(1)} %all-to-all-done.3, f32[]{:T(128)} %broadcast.2552), dimensions={1}, to_apply=%all_to_all.61.reduce_sub_computation | reduce | bytes 6291460 | tf_op jit(solution)/shard_map/all_to_all | solution.py:140
  877.3 6.5 reshape.1952
  883.8 4.9 copy.132
  888.7 2.4 bitcast_add_fusion.16
  891.1 14.3 %pad_maximum_fusion = f32[7,6,128,1024]{2,3,1,0:T(8,128)} fusion(f32[6,6,128,1024]{2,3,1,0:T(8,128)} %slice.388, f32[1,6,128,1024]{2,3,1,0:T(8,128)S(1)} %bitcast_add_fusion.16), kind=kLoop, calls=%fused_computation.409 | loop fusion | flops 5505024 | bytes 44040192 | tf_op jit(solution)/shard_map/concatenate | solution.py:142
  905.4 21.7 %copy.133 = f32[7,6,128,1024]{3,2,1,0:T(8,128)} copy(f32[7,6,128,1024]{2,3,1,0:T(8,128)} %pad_maximum_fusion) | data formatting | bytes 44040192 | tf_op jit(solution)/shard_map/concatenate | solution.py:142
  (770 shorter events, 155.3 us)
Async XLA Ops:
  1.5 23.5 %copy-start.2 = (f32[128,1024]{1,0:T(8,128)S(1)}, f32[128,1024]{1,0:T(8,128)}, u32[]{:S(2)}) copy-start(f32[128,1024]{1,0:T(8,128)} %param.8) | copy-start | bytes 1572868
  1.5 23.7 %copy-start.3 = (f32[128,1024]{1,0:T(8,128)S(1)}, f32[128,1024]{1,0:T(8,128)}, u32[]{:S(2)}) copy-start(f32[128,1024]{1,0:T(8,128)} %param.9) | copy-start | bytes 1572868
  1.5 23.9 %collective-permute-start = (f32[7,6,1,1024]{3,2,1,0:T(1,128)S(1)}, f32[7,6,1,1024]{3,2,1,0:T(1,128)S(1)}, u32[]{:S(2)}, u32[]{:S(2)}) collective-permute-start(f32[7,6,1,1024]{3,2,1,0:T(1,128)S(1)} %slice.307), channel_id=1, source_target_pairs={{0,1},{1,2},{2,3},{3,4},{4,5},{5,6},{6,7},{7,8},{8,9},{9,10},{10,1... | collective-permute-start | bytes 516104 | tf_op jit(solution)/shard_map/ppermute | solution.py:16
  25.2 10.7 %copy-start = (f32[128,1024]{0,1:T(8,128)}, f32[128,1024]{0,1:T(8,128)S(1)}, u32[]{:S(2)}) copy-start(f32[128,1024]{0,1:T(8,128)S(1)} %copy.107) | copy-start | bytes 1572868
  25.4 10.5 %copy-start.1 = (f32[128,1024]{0,1:T(8,128)}, f32[128,1024]{0,1:T(8,128)S(1)}, u32[]{:S(2)}) copy-start(f32[128,1024]{0,1:T(8,128)S(1)} %copy.112) | copy-start | bytes 1572868
  102.3 2.5 collective-permute-start.1
  158.5 101.3 %all-to-all-start = ((f32[6,128,1024]{1,0,2:T(8,128)}), f32[6,128,1024]{1,0,2:T(8,128)}, u32[]{:S(2)}, u32[]{:S(2)}) async-start(f32[6,128,1024]{1,0,2:T(8,128)} %copy.119), calls=%async_computation | async-start | bytes 8388608 | tf_op jit(solution)/shard_map/all_to_all | solution.py:114
  168.0 17.6 %copy-start.4 = (s32[32]{0:T(128)}, s32[32]{0:T(128)S(1)}, u32[]{:S(2)}) copy-start(s32[32]{0:T(128)S(1)} %get-tuple-element.513) | copy-start | bytes 388
  285.1 9.4 %copy-start.5 = (s32[32]{0:T(128)S(1)}, s32[32]{0:T(128)}, u32[]{:S(2)}) copy-start(s32[32]{0:T(128)} %copy-done.4) | copy-start | bytes 388
  289.4 185.9 %all-to-all-start.1 = ((f32[16,1,24576]{2,1,0:T(1,128)}), f32[16,1,24576]{2,1,0:T(1,128)S(1)}, u32[]{:S(2)}, u32[]{:S(2)}) async-start(f32[16,1,24576]{2,1,0:T(1,128)} %reshape.1947), calls=%async_computation.1 | async-start | bytes 3145728 | tf_op jit(solution)/shard_map/all_to_all | solution.py:131
  295.4 173.3 %copy-start.6 = (s32[32]{0:T(128)S(1)}, s32[32]{0:T(128)}, u32[]{:S(2)}) copy-start(s32[32]{0:T(128)} %copy-done.4) | copy-start | bytes 388
  295.4 173.4 %copy-start.7 = (f32[512]{0:T(512)S(1)}, f32[512]{0:T(512)}, u32[]{:S(2)}) copy-start(f32[512]{0:T(512)} %param.11) | copy-start | bytes 6148
  697.6 42.2 %all-to-all-start.2 = ((f32[16,1,24576]{2,1,0:T(1,128)}), f32[16,1,24576]{2,1,0:T(1,128)S(1)}, u32[]{:S(2)}, u32[]{:S(2)}) async-start(f32[16,1,24576]{2,1,0:T(1,128)} %reshape.1949), calls=%async_computation.2 | async-start | bytes 3145728 | tf_op jit(solution)/shard_map/all_to_all | solution.py:136
  791.5 75.0 %all-to-all-start.3 = ((f32[16,1,49152]{2,1,0:T(1,128)}), f32[16,1,49152]{2,1,0:T(1,128)S(1)}, u32[]{:S(2)}, u32[]{:S(2)}) async-start(f32[16,1,49152]{2,1,0:T(1,128)} %reshape.1951), calls=%async_computation.3 | async-start | bytes 6291456 | tf_op jit(solution)/shard_map/all_to_all | solution.py:140
where the time goes:
time: 936 us; the launch traced here: 927 us
  other arithmetic  284 us (30%)
  local copies, waits for them, and re-layouts  248 us (26%)
  matrix products  220 us (24%)
  waiting for transfers between devices  144 us (15%)
  starting transfers between devices  27.3 us (3%)
    dot_general x1, matrix products, body(): jnp.einsum('skj,cslj->skcl', legendre, weighted, precision=highest)  107 us
    while x480, other arithmetic  101 us
    dot_general x1, matrix products, body(): jnp.einsum('skj,skcl->cslj', legendre, scaled, precision=highest)  85.2 us
    sub x2, other arithmetic, advect(): cells - lon_courant * (cells - west_cells)  73.5 us
    all_to_all x1, waiting for transfers between devices, body(): lax.all_to_all(anomaly, 'band', split_axis=2, concat_axis=1, tiled=True)  70.2 us
    unnamed x26, local copies, waits for them, and re-layouts  66.9 us
    all_to_all x1, waiting for transfers between devices, body(): lax.all_to_all(band_increment, 'band', split_axis=1, concat_axis=2, tiled...  55.4 us
    dynamic_update_slice x32, local copies, waits for them, and re-layouts, legendre_table(): lax.scan(advance, (zero_row, zero_row, zero_row), (wave_rows.T, offset_ro...  47.4 us
  transfers between devices with their start and end apart: 6, of which 3 were waited for; matrix products, arithmetic and copies ran while one was open for 28% of the time, Pallas kernels for 0%

commit v1 on v0

v1 whole, which is shorter than its diff:
```python
import functools
import math

import jax
import jax.numpy as jnp
import numpy as np
from jax import lax
from jax.experimental import pallas as pl
from jax.experimental.pallas import tpu as pltpu
from jax.sharding import PartitionSpec as P

STEPS = 2
SHIFT = 44.0
GROUP = 8
ROWS = 16
VMEM = 56 * 1024 * 1024


def passed_along(value, axis, by):
    peers = lax.axis_size(axis)
    return lax.ppermute(value, axis, [(i, (i + by) % peers) for i in range(peers)])


def prepare(lon_ref, lat_ref, keep, south, lanes):
    first = lanes == 0
    for r in range(0, keep.shape[0], 8):
        cl = lon_ref[r : r + 8, :]
        ct = lat_ref[r : r + 8, :]
        keep[r : r + 8, :] = 1.0 - cl - ct
        south[r : r + 8, :] = jnp.where(first, 0.0, ct)


def two_steps(read, halo, edge_ref, lon_ref, keep, south, rows, lanes, emit):
    lat = keep.shape[1]
    top = rows == 0
    far = jnp.broadcast_to(halo[0:1, :], (8, lat))
    near = jnp.broadcast_to(halo[1:2, :], (8, lat))
    edge_lon = jnp.broadcast_to(edge_ref[0:1, :], (8, lat))
    edge_lat = jnp.broadcast_to(edge_ref[1:2, :], (8, lat))
    edge_keep = 1.0 - edge_lon - edge_lat
    edge_south = jnp.where(lanes == 0, 0.0, edge_lat)
    west0 = near
    west1 = edge_keep * near + edge_lon * far + edge_south * pltpu.roll(near, 1, 1)
    for r in range(0, keep.shape[0], 8):
        cells = read(r)
        ck = keep[r : r + 8, :]
        cs = south[r : r + 8, :]
        cl = lon_ref[r : r + 8, :]
        turned = pltpu.roll(cells, 1, 0)
        once = ck * cells + cl * jnp.where(top, west0, turned) + cs * pltpu.roll(cells, 1, 1)
        west0 = turned
        turned = pltpu.roll(once, 1, 0)
        twice = ck * once + cl * jnp.where(top, west1, turned) + cs * pltpu.roll(once, 1, 1)
        west1 = turned
        emit(r, twice)


def iotas(lat):
    return (
        lax.broadcasted_iota(jnp.int32, (8, lat), 0),
        lax.broadcasted_iota(jnp.int32, (8, lat), 1),
    )


def first_kernel(s_ref, h_ref, e_ref, lon_ref, lat_ref, f_ref, a_ref, t_ref, keep, south, diff):
    rows, lanes = iotas(keep.shape[1])

    @pl.when(pl.program_id(0) == 0)
    def _():
        prepare(lon_ref, lat_ref, keep, south, lanes)

    def emit(r, chunk):
        a_ref[0, r : r + 8, :] = chunk
        diff[r : r + 8, :] = f_ref[0, r : r + 8, :] - chunk

    two_steps(
        lambda r: s_ref[0, 0, r : r + 8, :], h_ref[0], e_ref, lon_ref, keep, south, rows, lanes, emit
    )
    t_ref[:, 0] = diff[...].T.reshape(t_ref.shape[0], t_ref.shape[2], t_ref.shape[3])


def rest_kernel(s_ref, h_ref, e_ref, lon_ref, lat_ref, o_ref, keep, south):
    rows, lanes = iotas(keep.shape[1])

    @pl.when((pl.program_id(0) == 0) & (pl.program_id(1) == 0))
    def _():
        prepare(lon_ref, lat_ref, keep, south, lanes)

    def one_level(i, carry):
        def emit(r, chunk):
            o_ref[0, i, r : r + 8, :] = chunk

        two_steps(
            lambda r: s_ref[0, i, r : r + 8, :],
            h_ref[0, i],
            e_ref,
            lon_ref,
            keep,
            south,
            rows,
            lanes,
            emit,
        )
        return carry

    lax.fori_loop(0, s_ref.shape[1], one_level, 0)


def last_kernel(a_ref, t_ref, b_ref, o_ref):
    lon, lat = a_ref.shape[1], a_ref.shape[2]
    o_ref[0, 0] = a_ref[0] + t_ref[:, 0].reshape(lat, lon).T


def table_kernel(start_ref, wave_ref, mu_ref, out_ref):
    half = mu_ref.shape[1]
    tiles = half // 128
    start = start_ref[...]
    mu = jnp.broadcast_to(mu_ref[...], (GROUP, half))
    wave = wave_ref[...]
    count = jnp.maximum(jnp.floor(start * (-1.0 / SHIFT)), 0.0)
    latest = jnp.exp(start + count * SHIFT)
    earlier = jnp.zeros_like(latest)
    before = jnp.ones_like(wave)

    def block(i, carry):
        latest, earlier, count, before = carry
        scale = jnp.exp(count * -SHIFT)
        for k in range(16):
            at = pl.multiple_of((i * 8 + k // 2) * GROUP, GROUP)
            row = latest * scale
            for c in range(tiles):
                out_ref[k % 2, c, pl.ds(at, GROUP), :] = row[:, c * 128 : (c + 1) * 128]
            offset = (i * 16 + (k + 1)).astype(jnp.float32)
            degree = wave + offset
            square = (4.0 * degree * degree - 1.0) / (offset * (degree + wave))
            factor = jnp.sqrt(square)
            older = factor / before
            before = factor
            wide = jnp.concatenate([factor] * tiles, axis=1)
            wide_old = jnp.concatenate([older] * tiles, axis=1)
            latest, earlier = wide * (mu * latest) - wide_old * earlier, latest
        grown = (jnp.maximum(jnp.abs(latest), jnp.abs(earlier)) > 1.0) & (count > 0.5)
        down = jnp.where(grown, math.exp(-SHIFT), 1.0)
        return latest * down, earlier * down, jnp.where(grown, count - 1.0, count), before

    lax.fori_loop(0, out_ref.shape[2] // (8 * GROUP), block, (latest, earlier, count, before))


def parts(x):
    high = x.astype(jnp.bfloat16)
    return high, (x - high.astype(jnp.float32)).astype(jnp.bfloat16)


def dot(a, b, dims):
    return lax.dot_general(a, b, (dims, ((), ())), preferred_element_type=jnp.float32)


def mirrored(x, flip):
    high, low = parts(x)
    both = ((1,), (0,))
    return dot(high, flip, both) + dot(low, flip, both)


def transform_kernel(first, stride, f_ref, p_ref, r_ref, q_ref, j_ref, o_ref, even, odd):
    half = q_ref.shape[1]
    flip = j_ref[...]
    quad = q_ref[...]
    north = f_ref[:, :half]
    turned = mirrored(f_ref[:, half:], flip)
    even[...] = (north + turned) * quad
    odd[...] = (north - turned) * quad
    length = p_ref.shape[2] // GROUP
    for m in range(GROUP):
        sums = []
        for p, side in ((0, even), (1, odd)):
            f_high, f_low = parts(side[m * ROWS : (m + 1) * ROWS, :])
            table = [
                p_ref[p, c, pl.ds(m, length, stride=GROUP), :] for c in range(p_ref.shape[1])
            ]
            p_high, p_low = parts(jnp.concatenate(table, axis=1))
            across, along = ((1,), (1,)), ((1,), (0,))
            pair = dot(jnp.concatenate([f_high, f_low], axis=0), p_high, across)
            coeffs = pair[:ROWS] + pair[ROWS:] + dot(f_high, p_low, across)
            at = (first + m) * stride
            c_high, c_low = parts(coeffs * r_ref[p : p + 1, at : at + length])
            pair = dot(jnp.concatenate([c_high, c_low], axis=0), p_high, along)
            sums.append(pair[:ROWS] + pair[ROWS:] + dot(c_high, p_low, along))
        o_ref[m * ROWS : (m + 1) * ROWS, :half] = sums[0] + sums[1]
        even[m * ROWS : (m + 1) * ROWS, :] = sums[0] - sums[1]
    o_ref[:, half:] = mirrored(even[...], flip)


def cost(flops, moved):
    return pl.CostEstimate(flops=int(flops), bytes_accessed=int(moved), transcendentals=0)


def body(state, courant_lon, courant_lat, reference_field, nudge_rate):
    fields, levels, lon, lat = state.shape
    bands = lax.axis_size("band")
    place = lax.axis_index("band")
    lon_total = lon * bands
    lat_local = lat // bands
    waves = nudge_rate.shape[0]
    wave_local = waves // bands
    groups = wave_local // GROUP
    half = lat // 2
    params = functools.partial(pltpu.CompilerParams, vmem_limit_bytes=VMEM)
    f32 = jnp.float32

    edges = passed_along(jnp.concatenate([courant_lon[-1:], courant_lat[-1:]], axis=0), "band", 1)
    halo0 = passed_along(state[0, :, -2:], "band", 1)
    halo1 = passed_along(state[1:, :, -2:], "band", 1)

    whole2 = lambda *_: (0, 0)
    courant_specs = [
        pl.BlockSpec((2, lat), whole2),
        pl.BlockSpec((lon, lat), whole2),
        pl.BlockSpec((lon, lat), whole2),
    ]
    coef_scratch = [pltpu.VMEM((lon, lat), f32), pltpu.VMEM((lon, lat), f32)]
    cells = levels * lon * lat
    advected0, turned = pl.pallas_call(
        first_kernel,
        grid=(levels,),
        in_specs=[
            pl.BlockSpec((1, 1, lon, lat), lambda v: (0, v, 0, 0)),
            pl.BlockSpec((1, 2, lat), lambda v: (v, 0, 0)),
            *courant_specs,
            pl.BlockSpec((1, lon, lat), lambda v: (v, 0, 0)),
        ],
        out_specs=[
            pl.BlockSpec((1, lon, lat), lambda v: (v, 0, 0)),
            pl.BlockSpec((bands, 1, lat_local, lon), lambda v: (0, v, 0, 0)),
        ],
        out_shape=[
            jax.ShapeDtypeStruct((levels, lon, lat), f32),
            jax.ShapeDtypeStruct((bands, levels, lat_local, lon), f32),
        ],
        scratch_shapes=[*coef_scratch, pltpu.VMEM((lon, lat), f32)],
        compiler_params=params(),
        cost_estimate=cost(cells * 14, cells * 16),
        name="advect_first",
    )(state, halo0, edges, courant_lon, courant_lat, reference_field)

    spread = lax.all_to_all(turned, "band", 0, 0, tiled=True)

    per = 3 if levels % 3 == 0 else 1
    partial = pl.pallas_call(
        rest_kernel,
        grid=(fields - 1, levels // per),
        in_specs=[
            pl.BlockSpec((1, per, lon, lat), lambda f, v: (f + 1, v, 0, 0)),
            pl.BlockSpec((1, per, 2, lat), lambda f, v: (f, v, 0, 0)),
            *courant_specs,
        ],
        out_specs=pl.BlockSpec((1, per, lon, lat), lambda f, v: (f + 1, v, 0, 0)),
        out_shape=jax.ShapeDtypeStruct(state.shape, f32),
        scratch_shapes=coef_scratch,
        compiler_params=params(),
        cost_estimate=cost((fields - 1) * cells * 14, (fields - 1) * cells * 8),
        name="advect_rest",
    )(state, halo1, edges, courant_lon, courant_lat)

    order = (np.arange(bands)[:, None] + bands * np.arange(wave_local)[None, :]).reshape(-1)
    angle = (order[:, None] * np.arange(lon_total)[None, :] % lon_total) * (2.0 * np.pi / lon_total)
    waves_np = np.stack([np.cos(angle), -np.sin(angle)], axis=1).reshape(2 * waves, lon_total)
    forward = jnp.asarray((waves_np / lon_total).astype(np.float32))
    doubling = np.repeat(np.where(order == 0, 1.0, 2.0), 2)[:, None]
    inverse = jnp.asarray((waves_np * doubling).astype(np.float32))
    theta = np.pi * (np.arange(half) + 0.5) / lat
    mu = jnp.asarray(np.cos(theta)[None].astype(np.float32))
    quad = jnp.asarray((np.sin(theta) * np.pi / lat)[None].astype(np.float32))
    log_sin = jnp.asarray(np.log(np.sin(theta)).astype(np.float32))
    k = np.arange(1, waves)
    norms = np.concatenate([[0.0], np.cumsum(np.log((2.0 * k + 1.0) / (2.0 * k)))])
    norms = norms.reshape(wave_local, bands).T.astype(np.float32)
    own_norm = lax.dynamic_slice_in_dim(jnp.asarray(norms), place, 1, 0)[0]
    own_wave = (place + bands * jnp.arange(wave_local)).astype(f32)
    starts = 0.5 * own_norm[:, None] + own_wave[:, None] * log_sin[None] - 0.5 * math.log(2.0)
    wide_wave = jnp.broadcast_to(own_wave[:, None], (wave_local, 128))
    flip = jnp.asarray(np.eye(half)[::-1].astype(np.float32)).astype(jnp.bfloat16)
    own_rate = lax.dynamic_slice_in_dim(
        jnp.concatenate([nudge_rate, jnp.zeros((waves + bands,), f32)]), place, 2 * waves, 0
    )

    own_rate = own_rate.reshape(waves, 2).T

    tables = []
    for g in range(groups):
        depth = waves - bands * GROUP * g
        depth = -(-depth // 16) * 16
        at = slice(g * GROUP, (g + 1) * GROUP)
        tables.append(
            pl.pallas_call(
                table_kernel,
                out_shape=jax.ShapeDtypeStruct((2, half // 128, depth // 2 * GROUP, 128), f32),
                compiler_params=params(),
                cost_estimate=cost(depth * GROUP * half * 8, depth * GROUP * half * 4),
                name="legendre_table",
            )(starts[at], wide_wave[at], mu)
        )

    fourier = lax.dot_general(
        forward.reshape(2 * waves, bands, lon),
        spread,
        (((1, 2), (0, 3)), ((), ())),
        precision=lax.Precision.HIGH,
    )
    fourier = fourier.reshape(bands, 2 * wave_local, levels * lat_local)
    owned = lax.all_to_all(fourier, "band", 0, 0, tiled=True)
    owned = owned.reshape(bands, wave_local, 2, levels, lat_local).transpose(1, 2, 3, 0, 4)
    owned = owned.reshape(wave_local, 2 * levels, lat)
    owned = jnp.pad(owned, ((0, 0), (0, ROWS - 2 * levels), (0, 0)))

    synth = []
    for g in range(groups):
        length = tables[g].shape[2] // GROUP
        block = owned[g * GROUP : (g + 1) * GROUP].reshape(GROUP * ROWS, lat)
        synth.append(
            pl.pallas_call(
                functools.partial(transform_kernel, g * GROUP, bands // 2),
                out_shape=jax.ShapeDtypeStruct((GROUP * ROWS, lat), f32),
                scratch_shapes=[pltpu.VMEM((GROUP * ROWS, half), f32)] * 2,
                compiler_params=params(),
                cost_estimate=cost(length * GROUP * half * 400, length * GROUP * half * 8),
                name="legendre_transform",
            )(block, tables[g], own_rate, quad, flip)
        )
    waves_out = jnp.concatenate(synth, axis=0).reshape(wave_local, ROWS, lat)[:, : 2 * levels]
    waves_out = waves_out.reshape(wave_local, 2, levels, bands, lat_local).transpose(3, 0, 1, 2, 4)
    waves_out = waves_out.reshape(bands, 2 * wave_local, levels * lat_local)
    gathered = lax.all_to_all(waves_out, "band", 0, 0, tiled=True)
    gathered = gathered.reshape(2 * waves, levels * lat_local)
    increment = lax.dot_general(
        gathered, inverse, (((0,), (0,)), ((), ())), precision=lax.Precision.HIGH
    )
    increment = increment.reshape(levels * lat_local, bands, lon).transpose(1, 0, 2)
    increment = increment.reshape(bands, levels, lat_local, lon)
    increment = lax.all_to_all(increment, "band", 0, 0, tiled=True)

    return pl.pallas_call(
        last_kernel,
        grid=(levels,),
        in_specs=[
            pl.BlockSpec((1, lon, lat), lambda v: (v, 0, 0)),
            pl.BlockSpec((bands, 1, lat_local, lon), lambda v: (0, v, 0, 0)),
            pl.BlockSpec(memory_space=pl.ANY),
        ],
        out_specs=pl.BlockSpec((1, 1, lon, lat), lambda v: (0, v, 0, 0)),
        out_shape=jax.ShapeDtypeStruct(state.shape, f32),
        input_output_aliases={2: 0},
        compiler_params=params(),
        cost_estimate=cost(cells, cells * 12),
        name="add_increment",
    )(advected0, increment, partial)


def solution(mesh):
    placed = (
        P("member", None, "band", None),
        P(("member", "band"), None),
        P(("member", "band"), None),
        P("member", "band", None),
        P(),
    )
    return jax.shard_map(
        body, mesh=mesh, in_specs=placed, out_specs=P("member", None, "band", None), check_vma=False
    )
```

time: 936 us -> 396 us (0.42)
  other arithmetic: 284 us -> 2.08 us
  local copies, waits for them, and re-layouts: 248 us -> 42.5 us
  matrix products: 220 us -> 22.4 us
  blocking collectives: 0 us -> 118 us
  Pallas kernels: 0 us -> 114 us
  waiting for transfers between devices: 144 us -> 80.6 us
  starting transfers between devices: 27.3 us -> 13.4 us
    dot_general x3 -> x2, matrix products: 207 us -> 22.4 us  [the longest x1 13.5 us: body(): lax.dot_general(gathered, inverse, (((0,), (0,)), ((), ())), precision=la...]
    all_to_all x4 -> x2, waiting for transfers between devices: 144 us -> 11 us  [the longest x1 11 us: body(): owned = lax.all_to_all(fourier, 'band', 0, 0, tiled=True)]
    all_to_all x0 -> x2, blocking collectives: none -> 118 us  [the longest x1 76.9 us: body(): spread = lax.all_to_all(turned, 'band', 0, 0, tiled=True)]
    pallas_call x0 -> x11, Pallas kernels: none -> 114 us  [the longest x4 39.8 us: body(): pl.pallas_call(functools.partial(transform_kernel, g * GROUP, bands // 2)...]
    while x480 -> x0, other arithmetic: 101 us -> none
    sub x3 -> x1, other arithmetic: 75.7 us -> 0.08 us  [body(): 0.5 * own_norm[:, None] + own_wave[:, None] * log_sin[None]]
    ppermute x2 -> x3, waiting for transfers between devices: 0.01 us -> 69.6 us  [passed_along(): lax.ppermute(value, axis, [(i, (i + by) % peers) for i in range(peers)])]
    unnamed x26 -> x19, local copies, waits for them, and re-layouts: 66.9 us -> 5.64 us
  transfers between devices with their start and end apart: 6 -> 5, of which waited for: 3 -> 3; matrix products, arithmetic and copies ran while one was open for 28% -> 2% of each run, Pallas kernels for 0% -> 15%
where the time goes in v1:
time: 396 us; the launch traced here: 393 us
  blocking collectives  118 us (30%)
  Pallas kernels  114 us (29%)
  waiting for transfers between devices  80.6 us (20%)
  local copies, waits for them, and re-layouts  42.5 us (11%)
  matrix products  22.4 us (6%)
  starting transfers between devices  13.4 us (3%)
    all_to_all x1, blocking collectives, body(): spread = lax.all_to_all(turned, 'band', 0, 0, tiled=True)  76.9 us
    ppermute x3, waiting for transfers between devices, passed_along(): lax.ppermute(value, axis, [(i, (i + by) % peers) for i in range(peers)])  69.6 us
    all_to_all x1, blocking collectives, body(): gathered = lax.all_to_all(waves_out, 'band', 0, 0, tiled=True)  40.8 us
    pallas_call x4, Pallas kernels, body(): pl.pallas_call(functools.partial(transform_kernel, g * GROUP, bands // 2)...  39.8 us
    pallas_call x1, Pallas kernels, body(): pl.pallas_call(rest_kernel, grid=(fields - 1, levels // per), in_specs=[p...  37.7 us
    pallas_call x4, Pallas kernels, body(): pl.pallas_call(table_kernel, out_shape=jax.ShapeDtypeStruct((2, half // 1...  20 us
    dot_general x1, matrix products, body(): lax.dot_general(gathered, inverse, (((0,), (0,)), ((), ())), precision=la...  13.5 us
    all_to_all x1, waiting for transfers between devices, body(): owned = lax.all_to_all(fourier, 'band', 0, 0, tiled=True)  11 us
  transfers between devices with their start and end apart: 5, of which 3 were waited for; matrix products, arithmetic and copies ran while one was open for 2% of the time, Pallas kernels for 15%

profile of v1, /device:TPU:15, one launch (start us, length us, event | category | flops | bytes accessed | tf_op | source)
XLA Modules:
  0.0 393.2 jit_solution(12752252781114948642)
XLA Ops:
  0.0 0.9 slice_bitcast_fusion
  1.0 1.9 collective-permute-start
  2.8 0.8 slice.68
  3.6 0.8 slice.69
  4.3 0.1 collective-permute-start.1
  4.4 1.2 collective-permute-done.1.e_ref
  5.6 0.0 collective-permute-done.h_ref
  5.6 0.6 copy-done.6
  6.2 0.6 copy-done.5
  6.8 10.7 %advect_first.1 = (f32[6,128,1024]{2,1,0:T(8,128)}, f32[16,6,64,128]{3,2,1,0:T(8,128)}) custom-call(f32[7,6,128,1024]{3,2,1,0:T(8,128)} %s_ref.3, f32[6,2,1024]{2,1,0:T(2,128)} %copy-done.5, f32[2,1024]{1,0:T(2,128)} %copy-done.6, f32[128,1024]{1,0:T(8,128)} %lon_ref.3, f32[128,1024]{1,0:T(8,128)} %lat_ref.3, f32[6,128,1024]{2,1,0:T(8,128)} %f_ref.1), custom_call_target="tpu_custom_call" | custom-call | flops 11010048 | bytes 12582912 | tf_op jit(solution)/shard_map/advect_first/pallas_call | solution.py:222
  17.5 76.9 %all_to_all.20 = f32[16,6,64,128]{3,2,1,0:T(8,128)S(1)} all-to-all(f32[16,6,64,128]{3,2,1,0:T(8,128)} %get-tuple-element.8), channel_id=1, replica_groups=mesh['member'=2,'band'=16] {'band'}, dimensions={0} | all-to-all | bytes 6291456 | tf_op jit(solution)/shard_map/all_to_all | solution.py:245
  94.4 8.9 %fusion.2 = f32[1024,6,64]{0,2,1:T(8,128)} fusion(f32[16,6,64,128]{3,2,1,0:T(8,128)S(1)} %all_to_all.20, f32[1024,16,128,1]{2,0,1,3:T(8,128)} %constant.49), kind=kOutput, calls=%fused_computation.7 | convolution fusion | flops 4831838208 | bytes 13107200 | tf_op jit(solution)/shard_map/dot_general | solution.py:303
  103.3 2.5 reshape.73
  105.8 0.0 copy-start.8
  105.8 0.0 copy-start.7
  105.8 2.0 copy.29
  107.9 5.0 %all-to-all-start.1 = ((f32[16,64,384]{2,1,0:T(8,128)}), f32[16,64,384]{2,1,0:T(8,128)S(1)}, u32[]{:S(2)}, u32[]{:S(2)}) async-start(f32[16,64,384]{2,1,0:T(8,128)} %copy.29), calls=%async_computation.1 | async-start | bytes 3145728 | tf_op jit(solution)/shard_map/all_to_all | solution.py:310
  112.9 0.0 copy-done.8
  112.9 0.1 pad_dynamic-slice_fusion
  112.9 0.2 reshape.77
  113.1 0.7 copy.32
  113.9 0.7 multiply_bitcast_fusion
  114.6 0.1 slice_bitcast_fusion.4
  114.6 0.0 copy-done.7
  114.6 0.1 add_add_fusion
  114.7 0.6 fusion.5
  115.3 0.7 broadcast_in_dim.18.wave_ref
  116.0 2.8 legendre_table.7.p_ref
  118.8 0.7 broadcast_in_dim.17.wave_ref
  119.5 4.3 %legendre_table.6.p_ref = f32[2,4,1024,128]{3,2,1,0:T(8,128)} custom-call(f32[8,512]{1,0:T(8,128)} %get-tuple-element.15.start_ref, f32[8,128]{1,0:T(8,128)} %broadcast_in_dim.17.wave_ref, f32[1,512]{1,0:T(1,128)} %constant.35.clone.mu_ref), custom_call_target="tpu_custom_call" | custom-call | flops 8388608 | bytes 4194304 | tf_op jit(solution)/shard_map/legendre_table/pallas_call | solution.py:294
  123.8 0.7 broadcast_in_dim.16.wave_ref
  124.4 5.7 %legendre_table.5.p_ref = f32[2,4,1536,128]{3,2,1,0:T(8,128)} custom-call(f32[8,512]{1,0:T(8,128)} %get-tuple-element.16.start_ref, f32[8,128]{1,0:T(8,128)} %broadcast_in_dim.16.wave_ref, f32[1,512]{1,0:T(1,128)} %constant.35.clone.mu_ref), custom_call_target="tpu_custom_call" | custom-call | flops 12582912 | bytes 6291456 | tf_op jit(solution)/shard_map/legendre_table/pallas_call | solution.py:294
  130.2 0.7 broadcast_in_dim.15.wave_ref
  130.8 7.2 %legendre_table.4.p_ref = f32[2,4,2048,128]{3,2,1,0:T(8,128)} custom-call(f32[8,512]{1,0:T(8,128)} %get-tuple-element.13.start_ref, f32[8,128]{1,0:T(8,128)} %broadcast_in_dim.15.wave_ref, f32[1,512]{1,0:T(1,128)} %constant.35.clone.mu_ref), custom_call_target="tpu_custom_call" | custom-call | flops 16777216 | bytes 8388608 | tf_op jit(solution)/shard_map/legendre_table/pallas_call | solution.py:294
  138.0 11.0 %all-to-all-done.1 = f32[16,64,384]{2,1,0:T(8,128)S(1)} async-done(((f32[16,64,384]{2,1,0:T(8,128)}), f32[16,64,384]{2,1,0:T(8,128)S(1)}, u32[]{:S(2)}, u32[]{:S(2)}) %all-to-all-start.1) | async-done | bytes 1572896 | tf_op jit(solution)/shard_map/all_to_all | solution.py:310
  149.0 2.5 reshape.74
  151.5 4.0 %copy.30 = f32[32,2,6,16,64]{4,3,0,2,1:T(8,128)S(1)} copy(f32[32,2,6,16,64]{4,2,1,0,3:T(8,128)} %bitcast.49) | data formatting | bytes 3145728 | tf_op jit(solution)/shard_map/transpose | solution.py:311
  155.6 1.8 reshape.75
  157.4 1.6 pad_slice_fusion.3
  159.0 1.1 copy.31
  160.1 1.1 copy.33
  161.2 1.1 copy.34
  162.3 1.2 copy.35
  163.4 8.8 %legendre_transform.6 = f32[128,1024]{1,0:T(8,128)} custom-call(f32[128,1024]{1,0:T(8,128)} %bitcast.55, f32[2,4,1024,128]{3,2,1,0:T(8,128)} %legendre_table.6.p_ref, f32[2,512]{1,0:T(2,128)} %bitcast.57, f32[1,512]{1,0:T(1,128)} %constant.36.clone.q_ref, bf16[512,512]{1,0:T(8,128)(2,1)} %constant.46.j_ref), custom_call_target="tpu_custom_call" | custom-call | flops 209715200 | bytes 4194304 | tf_op jit(solution)/shard_map/legendre_transform/pallas_call | solution.py:320
  172.2 6.8 %legendre_transform.7 = f32[128,1024]{1,0:T(8,128)} custom-call(f32[128,1024]{1,0:T(8,128)} %bitcast.56, f32[2,4,512,128]{3,2,1,0:T(8,128)} %legendre_table.7.p_ref, f32[2,512]{1,0:T(2,128)} %bitcast.58, f32[1,512]{1,0:T(1,128)} %constant.36.clone.q_ref, bf16[512,512]{1,0:T(8,128)(2,1)} %constant.46.j_ref), custom_call_target="tpu_custom_call" | custom-call | flops 104857600 | bytes 2097152 | tf_op jit(solution)/shard_map/legendre_transform/pallas_call | solution.py:320
  179.1 10.9 %legendre_transform.5 = f32[128,1024]{1,0:T(8,128)} custom-call(f32[128,1024]{1,0:T(8,128)} %bitcast.54, f32[2,4,1536,128]{3,2,1,0:T(8,128)} %legendre_table.5.p_ref, f32[2,512]{1,0:T(2,128)} %bitcast.59, f32[1,512]{1,0:T(1,128)} %constant.36.clone.q_ref, bf16[512,512]{1,0:T(8,128)(2,1)} %constant.46.j_ref), custom_call_target="tpu_custom_call" | custom-call | flops 314572800 | bytes 6291456 | tf_op jit(solution)/shard_map/legendre_transform/pallas_call | solution.py:320
  190.0 13.2 %legendre_transform.4 = f32[128,1024]{1,0:T(8,128)} custom-call(f32[128,1024]{1,0:T(8,128)} %bitcast.53, f32[2,4,2048,128]{3,2,1,0:T(8,128)} %legendre_table.4.p_ref, f32[2,512]{1,0:T(2,128)} %bitcast.60, f32[1,512]{1,0:T(1,128)} %constant.36.clone.q_ref, bf16[512,512]{1,0:T(8,128)(2,1)} %constant.46.j_ref), custom_call_target="tpu_custom_call" | custom-call | flops 419430400 | bytes 8388608 | tf_op jit(solution)/shard_map/legendre_transform/pallas_call | solution.py:320
  203.2 0.0 copy-done.2
  203.2 1.3 pad_maximum_fusion
  204.5 2.1 copy.42
  206.5 2.5 reshape.82
  209.1 3.9 copy.37
  213.0 3.3 reshape.83
  216.3 40.8 %all_to_all.21 = f32[16,64,384]{2,1,0:T(8,128)S(1)} all-to-all(f32[16,64,384]{2,1,0:T(8,128)S(1)} %reshape.83), channel_id=1, replica_groups=mesh['member'=2,'band'=16] {'band'}, dimensions={0} | all-to-all | bytes 3145728 | tf_op jit(solution)/shard_map/all_to_all | solution.py:332
  257.0 13.5 %fusion.6 = f32[384,16,128]{2,0,1:T(8,128)} fusion(f32[1024,384,1]{1,0,2:T(8,128)S(1)} %bitcast.52, f32[16,128,1024]{2,1,0:T(8,128)} %constant.48), kind=kOutput, calls=%fused_computation.20 | convolution fusion | flops 4831838208 | bytes 13107200 | tf_op jit(solution)/shard_map/dot_general | solution.py:334
  270.5 5.0 %all-to-all-start.3 = ((f32[16,6,64,128]{3,2,1,0:T(8,128)}), f32[16,6,64,128]{3,2,1,0:T(8,128)S(1)}, u32[]{:S(2)}, u32[]{:S(2)}) async-start(f32[16,6,64,128]{3,2,1,0:T(8,128)} %bitcast.20), calls=%async_computation.3 | async-start | bytes 6291456 | tf_op jit(solution)/shard_map/all_to_all | solution.py:339
  275.6 1.4 slice.87
  277.0 1.5 collective-permute-start.2
  278.5 68.4 %collective-permute-done.2.h_ref = f32[6,6,2,1024]{3,2,1,0:T(2,128)S(1)} collective-permute-done((f32[6,6,2,1024]{3,2,1,0:T(2,128)S(1)}, f32[6,6,2,1024]{3,2,1,0:T(2,128)S(1)}, u32[]{:S(2)}, u32[]{:S(2)}) %collective-permute-start.2) | collective-permute-done | bytes 294944 | tf_op jit(solution)/shard_map/ppermute | solution.py:21
  346.9 0.7 copy-done.4
  347.6 37.7 %advect_rest.1.b_ref = f32[7,6,128,1024]{3,2,1,0:T(8,128)} custom-call(f32[7,6,128,1024]{3,2,1,0:T(8,128)} %s_ref.3, f32[6,6,2,1024]{3,2,1,0:T(2,128)} %copy-done.4, f32[2,1024]{1,0:T(2,128)} %copy-done.6, f32[128,1024]{1,0:T(8,128)} %lon_ref.3, f32[128,1024]{1,0:T(8,128)} %lat_ref.3), custom_call_target="tpu_custom_call" | custom-call | flops 66060288 | bytes 37748736 | tf_op jit(solution)/shard_map/advect_rest/pallas_call | solution.py:248
  385.3 0.0 all-to-all-done.3.t_ref
  385.3 1.6 copy-done
  386.9 6.3 %add_increment.1 = f32[7,6,128,1024]{3,2,1,0:T(8,128)} custom-call(f32[6,128,1024]{2,1,0:T(8,128)} %get-tuple-element.7.a_ref, f32[16,6,64,128]{3,2,1,0:T(8,128)} %copy-done, f32[7,6,128,1024]{3,2,1,0:T(8,128)} %advect_rest.1.b_ref), custom_call_target="tpu_custom_call", output_to_operand_aliasing={{}: (2, {})} | custom-call | flops 786432 | bytes 9437184 | tf_op jit(solution)/shard_map/add_increment/pallas_call | solution.py:341
  (12 shorter events, 0.0 us)
Async XLA Ops:
  1.0 4.6 %collective-permute-start = (f32[6,2,1024]{2,1,0:T(2,128)S(1)}, f32[6,2,1024]{2,1,0:T(2,128)S(1)}, u32[]{:S(2)}, u32[]{:S(2)}) collective-permute-start(f32[6,2,1024]{2,1,0:T(2,128)S(1)} %slice_bitcast_fusion), channel_id=1, source_target_pairs={{0,1},{1,2},{2,3},{3,4},{4,5},{5,6},{6,7},{7,8},{8,9},{9,10},{10,1... | collective-permute-start | bytes 147464 | tf_op jit(solution)/shard_map/ppermute | solution.py:21
  4.3 1.2 collective-permute-start.1
  5.6 0.6 copy-start.6
  6.2 0.6 copy-start.5
  105.8 7.0 %copy-start.8 = (f32[512]{0:T(512)S(1)}, f32[512]{0:T(512)}, u32[]{:S(2)}) copy-start(f32[512]{0:T(512)} %param.16) | copy-start | bytes 6148
  105.8 8.8 %copy-start.7 = (f32[512]{0:T(512)S(1)}, f32[512]{0:T(512)}, u32[]{:S(2)}) copy-start(f32[512]{0:T(512)} %constant.37.clone) | copy-start | bytes 6148
  107.9 41.2 %all-to-all-start.1 = ((f32[16,64,384]{2,1,0:T(8,128)}), f32[16,64,384]{2,1,0:T(8,128)S(1)}, u32[]{:S(2)}, u32[]{:S(2)}) async-start(f32[16,64,384]{2,1,0:T(8,128)} %copy.29), calls=%async_computation.1 | async-start | bytes 3145728 | tf_op jit(solution)/shard_map/all_to_all | solution.py:310
  190.0 13.2 %copy-start.1 = (f32[128,1024]{1,0:T(8,128)S(1)}, f32[128,1024]{1,0:T(8,128)}, u32[]{:S(2)}) copy-start(f32[128,1024]{1,0:T(8,128)} %legendre_transform.6) | copy-start | bytes 1572868
  190.0 13.2 %copy-start.2 = (f32[128,1024]{1,0:T(8,128)S(1)}, f32[128,1024]{1,0:T(8,128)}, u32[]{:S(2)}) copy-start(f32[128,1024]{1,0:T(8,128)} %legendre_transform.5) | copy-start | bytes 1572868
  190.0 13.2 %copy-start.3 = (f32[128,1024]{1,0:T(8,128)S(1)}, f32[128,1024]{1,0:T(8,128)}, u32[]{:S(2)}) copy-start(f32[128,1024]{1,0:T(8,128)} %legendre_transform.7) | copy-start | bytes 1572868
  270.5 114.7 %all-to-all-start.3 = ((f32[16,6,64,128]{3,2,1,0:T(8,128)}), f32[16,6,64,128]{3,2,1,0:T(8,128)S(1)}, u32[]{:S(2)}, u32[]{:S(2)}) async-start(f32[16,6,64,128]{3,2,1,0:T(8,128)} %bitcast.20), calls=%async_computation.3 | async-start | bytes 6291456 | tf_op jit(solution)/shard_map/all_to_all | solution.py:339
  277.0 69.9 %collective-permute-start.2 = (f32[6,6,2,1024]{3,2,1,0:T(2,128)S(1)}, f32[6,6,2,1024]{3,2,1,0:T(2,128)S(1)}, u32[]{:S(2)}, u32[]{:S(2)}) collective-permute-start(f32[6,6,2,1024]{3,2,1,0:T(2,128)S(1)} %slice.87), channel_id=1, source_target_pairs={{0,1},{1,2},{2,3},{3,4},{4,5},{5,6},{6,7},{7,8},{8,9},{9,10},{10,1... | collective-permute-start | bytes 884744 | tf_op jit(solution)/shard_map/ppermute | solution.py:21
  346.9 0.7 copy-start.4
  385.3 1.6 copy-start

commit v2 on v1

--- a/solution.py
+++ b/solution.py
@@ -161,33 +161,68 @@
     return dot(high, flip, both) + dot(low, flip, both)
 
 
-def transform_kernel(first, stride, f_ref, p_ref, r_ref, q_ref, j_ref, o_ref, even, odd):
+def transform_kernel(firsts, stride, levels, *refs):
+    f_ref, *p_refs = refs[: 1 + len(firsts)]
+    r_ref, q_ref, j_ref, o_ref, even, odd = refs[1 + len(firsts) :]
+    bands, width = f_ref.shape[0], f_ref.shape[2] // levels
     half = q_ref.shape[1]
+    tiles = half // 128
+    used = 2 * levels * GROUP
+    pair_rows = 2 * GROUP
     flip = j_ref[...]
     quad = q_ref[...]
-    north = f_ref[:, :half]
-    turned = mirrored(f_ref[:, half:], flip)
-    even[...] = (north + turned) * quad
-    odd[...] = (north - turned) * quad
-    length = p_ref.shape[2] // GROUP
-    for m in range(GROUP):
-        sums = []
-        for p, side in ((0, even), (1, odd)):
-            f_high, f_low = parts(side[m * ROWS : (m + 1) * ROWS, :])
-            table = [
-                p_ref[p, c, pl.ds(m, length, stride=GROUP), :] for c in range(p_ref.shape[1])
-            ]
-            p_high, p_low = parts(jnp.concatenate(table, axis=1))
-            across, along = ((1,), (1,)), ((1,), (0,))
-            pair = dot(jnp.concatenate([f_high, f_low], axis=0), p_high, across)
-            coeffs = pair[:ROWS] + pair[ROWS:] + dot(f_high, p_low, across)
-            at = (first + m) * stride
-            c_high, c_low = parts(coeffs * r_ref[p : p + 1, at : at + length])
-            pair = dot(jnp.concatenate([c_high, c_low], axis=0), p_high, along)
-            sums.append(pair[:ROWS] + pair[ROWS:] + dot(c_high, p_low, along))
-        o_ref[m * ROWS : (m + 1) * ROWS, :half] = sums[0] + sums[1]
-        even[m * ROWS : (m + 1) * ROWS, :] = sums[0] - sums[1]
-    o_ref[:, half:] = mirrored(even[...], flip)
+    across, along = ((1,), (1,)), ((1,), (0,))
+    for number, (first, p_ref) in enumerate(zip(firsts, p_refs)):
+        here = slice(number * pair_rows, (number + 1) * pair_rows)
+        whole = jnp.concatenate(
+            [
+                jnp.concatenate(
+                    [f_ref[s, here, v * width : (v + 1) * width] for s in range(bands)], axis=1
+                )
+                for v in range(levels)
+            ],
+            axis=0,
+        )
+        north = whole[:, :half]
+        turned = mirrored(whole[:, half:], flip)
+        plus = (north + turned) * quad
+        minus = (north - turned) * quad
+        for c in range(tiles):
+            even[c, :used, :] = plus[:, c * 128 : (c + 1) * 128]
+            odd[c, :used, :] = minus[:, c * 128 : (c + 1) * 128]
+            if used < GROUP * ROWS:
+                even[c, used:, :] = jnp.zeros((GROUP * ROWS - used, 128), jnp.float32)
+                odd[c, used:, :] = jnp.zeros((GROUP * ROWS - used, 128), jnp.float32)
+        length = p_ref.shape[2] // GROUP
+        for m in range(GROUP):
+            sums = []
+            for p, side in ((0, even), (1, odd)):
+                rows = [side[c, pl.ds(m, ROWS, stride=GROUP), :] for c in range(tiles)]
+                f_high, f_low = parts(jnp.concatenate(rows, axis=1))
+                table = [p_ref[p, c, pl.ds(m, length, stride=GROUP), :] for c in range(tiles)]
+                p_high, p_low = parts(jnp.concatenate(table, axis=1))
+                pair = dot(jnp.concatenate([f_high, f_low], axis=0), p_high, across)
+                coeffs = pair[:ROWS] + pair[ROWS:] + dot(f_high, p_low, across)
+                at = (first + m) * stride
+                c_high, c_low = parts(coeffs * r_ref[p : p + 1, at : at + length])
+                pair = dot(jnp.concatenate([c_high, c_low], axis=0), p_high, along)
+                sums.append(pair[:ROWS] + pair[ROWS:] + dot(c_high, p_low, along))
+            plus = sums[0] + sums[1]
+            minus = sums[0] - sums[1]
+            for c in range(tiles):
+                even[c, pl.ds(m, ROWS, stride=GROUP), :] = plus[:, c * 128 : (c + 1) * 128]
+                odd[c, pl.ds(m, ROWS, stride=GROUP), :] = minus[:, c * 128 : (c + 1) * 128]
+        north = jnp.concatenate([even[c, :used, :] for c in range(tiles)], axis=1)
+        south = jnp.concatenate([odd[c, :used, :] for c in range(tiles)], axis=1)
+        whole = jnp.concatenate([north, mirrored(south, flip)], axis=1)
+        for s in range(bands):
+            o_ref[s, here, :] = jnp.concatenate(
+                [
+                    whole[v * pair_rows : (v + 1) * pair_rows, s * width : (s + 1) * width]
+                    for v in range(levels)
+                ],
+                axis=1,
+            )
 
 
 def cost(flops, moved):
@@ -210,6 +245,7 @@
     edges = passed_along(jnp.concatenate([courant_lon[-1:], courant_lat[-1:]], axis=0), "band", 1)
     halo0 = passed_along(state[0, :, -2:], "band", 1)
     halo1 = passed_along(state[1:, :, -2:], "band", 1)
+    edges, halo0, halo1 = lax.optimization_barrier((edges, halo0, halo1))
 
     whole2 = lambda *_: (0, 0)
     courant_specs = [
@@ -261,12 +297,21 @@
         name="advect_rest",
     )(state, halo1, edges, courant_lon, courant_lat)
 
-    order = (np.arange(bands)[:, None] + bands * np.arange(wave_local)[None, :]).reshape(-1)
-    angle = (order[:, None] * np.arange(lon_total)[None, :] % lon_total) * (2.0 * np.pi / lon_total)
-    waves_np = np.stack([np.cos(angle), -np.sin(angle)], axis=1).reshape(2 * waves, lon_total)
-    forward = jnp.asarray((waves_np / lon_total).astype(np.float32))
-    doubling = np.repeat(np.where(order == 0, 1.0, 2.0), 2)[:, None]
-    inverse = jnp.asarray((waves_np * doubling).astype(np.float32))
+    chunks = [
+        sorted({g, groups - 1 - g}) for g in range((groups + 1) // 2)
+    ]
+    forward, inverse = [], []
+    for chunk in chunks:
+        steps = np.asarray(chunk)[:, None, None] * GROUP + np.arange(GROUP)[None, None, :]
+        steps = np.broadcast_to(steps, (len(chunk), 2, GROUP)).reshape(-1)
+        part = np.broadcast_to(np.arange(2)[None, :, None], (len(chunk), 2, GROUP)).reshape(-1)
+        order = (np.arange(bands)[:, None] + bands * steps[None, :]).reshape(-1)
+        part = np.tile(part, bands)[:, None]
+        angle = (order[:, None] * np.arange(lon_total)[None, :] % lon_total) * (2 * np.pi / lon_total)
+        values = np.where(part == 0, np.cos(angle), -np.sin(angle))
+        doubling = np.where(order == 0, 1.0, 2.0)[:, None]
+        forward.append(jnp.asarray((values / lon_total).astype(np.float32)))
+        inverse.append(jnp.asarray((values * doubling).astype(np.float32)))
     theta = np.pi * (np.arange(half) + 0.5) / lat
     mu = jnp.asarray(np.cos(theta)[None].astype(np.float32))
     quad = jnp.asarray((np.sin(theta) * np.pi / lat)[None].astype(np.float32))
@@ -300,40 +345,36 @@
             )(starts[at], wide_wave[at], mu)
         )
 
-    fourier = lax.dot_general(
-        forward.reshape(2 * waves, bands, lon),
-        spread,
-        (((1, 2), (0, 3)), ((), ())),
-        precision=lax.Precision.HIGH,
-    )
-    fourier = fourier.reshape(bands, 2 * wave_local, levels * lat_local)
-    owned = lax.all_to_all(fourier, "band", 0, 0, tiled=True)
-    owned = owned.reshape(bands, wave_local, 2, levels, lat_local).transpose(1, 2, 3, 0, 4)
-    owned = owned.reshape(wave_local, 2 * levels, lat)
-    owned = jnp.pad(owned, ((0, 0), (0, ROWS - 2 * levels), (0, 0)))
-
-    synth = []
-    for g in range(groups):
-        length = tables[g].shape[2] // GROUP
-        block = owned[g * GROUP : (g + 1) * GROUP].reshape(GROUP * ROWS, lat)
-        synth.append(
-            pl.pallas_call(
-                functools.partial(transform_kernel, g * GROUP, bands // 2),
-                out_shape=jax.ShapeDtypeStruct((GROUP * ROWS, lat), f32),
-                scratch_shapes=[pltpu.VMEM((GROUP * ROWS, half), f32)] * 2,
-                compiler_params=params(),
-                cost_estimate=cost(length * GROUP * half * 400, length * GROUP * half * 8),
-                name="legendre_transform",
-            )(block, tables[g], own_rate, quad, flip)
+    spread, *tables = lax.optimization_barrier((spread, *tables))
+    rows = [2 * GROUP * len(chunk) for chunk in chunks]
+    increment = 0.0
+    for n, chunk in enumerate(chunks):
+        fourier = lax.dot_general(
+            forward[n].reshape(bands * rows[n], bands, lon),
+            spread,
+            (((1, 2), (0, 3)), ((), ())),
+            precision=lax.Precision.HIGH,
         )
-    waves_out = jnp.concatenate(synth, axis=0).reshape(wave_local, ROWS, lat)[:, : 2 * levels]
-    waves_out = waves_out.reshape(wave_local, 2, levels, bands, lat_local).transpose(3, 0, 1, 2, 4)
-    waves_out = waves_out.reshape(bands, 2 * wave_local, levels * lat_local)
-    gathered = lax.all_to_all(waves_out, "band", 0, 0, tiled=True)
-    gathered = gathered.reshape(2 * waves, levels * lat_local)
-    increment = lax.dot_general(
-        gathered, inverse, (((0,), (0,)), ((), ())), precision=lax.Precision.HIGH
-    )
+        fourier = fourier.reshape(bands, rows[n], levels * lat_local)
+        owned = lax.all_to_all(fourier, "band", 0, 0, tiled=True)
+        depth = sum(tables[g].shape[2] for g in chunk)
+        synth = pl.pallas_call(
+            functools.partial(
+                transform_kernel, tuple(g * GROUP for g in chunk), bands // 2, levels
+            ),
+            out_shape=jax.ShapeDtypeStruct(owned.shape, f32),
+            scratch_shapes=[pltpu.VMEM((half // 128, GROUP * ROWS, 128), f32)] * 2,
+            compiler_params=params(),
+            cost_estimate=cost(depth * half * 600, depth * half * 8),
+            name="legendre_transform",
+        )(owned, *[tables[g] for g in chunk], own_rate, quad, flip)
+        gathered = lax.all_to_all(synth, "band", 0, 0, tiled=True)
+        increment = increment + lax.dot_general(
+            gathered.reshape(bands * rows[n], levels * lat_local),
+            inverse[n],
+            (((0,), (0,)), ((), ())),
+            precision=lax.Precision.HIGH,
+        )
     increment = increment.reshape(levels * lat_local, bands, lon).transpose(1, 0, 2)
     increment = increment.reshape(bands, levels, lat_local, lon)
     increment = lax.all_to_all(increment, "band", 0, 0, tiled=True)

time: 396 us -> 298 us (0.75)
  blocking collectives: 118 us -> 0 us
  waiting for transfers between devices: 80.6 us -> 105 us
  starting transfers between devices: 13.4 us -> 36.7 us
  local copies, waits for them, and re-layouts: 42.5 us -> 21.6 us
    all_to_all x2 -> x0, blocking collectives: 118 us -> none  [the longest x1 76.9 us: body(): spread = lax.all_to_all(turned, 'band', 0, 0, tiled=True)]
    ppermute x3, waiting for transfers between devices: 69.6 us -> 0.8 us  [passed_along(): lax.ppermute(value, axis, [(i, (i + by) % peers) for i in range(peers)])]
    all_to_all x0 -> x3, waiting for transfers between devices: none -> 61.6 us  [the longest x1 45.8 us: body(): spread = lax.all_to_all(turned, 'band', 0, 0, tiled=True)]
    all_to_all x1, waiting for transfers between devices: 0.01 us -> 32.2 us  [body(): increment = lax.all_to_all(increment, 'band', 0, 0, tiled=True)]
    all_to_all x0 -> x3, starting transfers between devices: none -> 18.3 us  [the longest x2 10.9 us: body(): gathered = lax.all_to_all(synth, 'band', 0, 0, tiled=True)]
    reshape x6 -> x3, local copies, waits for them, and re-layouts: 14.7 us -> 6.09 us  [the longest x2 4.08 us: body(): fourier = fourier.reshape(bands, rows[n], levels * lat_local)]
    transpose x2 -> x0, local copies, waits for them, and re-layouts: 7.91 us -> none  [the longest x1 4.01 us: body(): owned.reshape(bands, wave_local, 2, levels, lat_local)]
    slice x5 -> x0, local copies, waits for them, and re-layouts: 6.05 us -> none  [body(): block = owned[g * GROUP:(g + 1) * GROUP].reshape(GROUP * ROWS, lat)]
  transfers between devices with their start and end apart: 5 -> 9, of which waited for: 3 -> 7; matrix products, arithmetic and copies ran while one was open for 2% -> 7% of each run, Pallas kernels for 15% -> 32%
where the time goes in v2:
time: 298 us; the launch traced here: 296 us
  Pallas kernels  111 us (37%)
  waiting for transfers between devices  105 us (35%)
  starting transfers between devices  36.7 us (12%)
  local copies, waits for them, and re-layouts  21.6 us (7%)
  matrix products  21 us (7%)
    all_to_all x1, waiting for transfers between devices, body(): spread = lax.all_to_all(turned, 'band', 0, 0, tiled=True)  45.8 us
    pallas_call x1, Pallas kernels, body(): pl.pallas_call(rest_kernel, grid=(fields - 1, levels // per), in_specs=[p...  37.7 us
    pallas_call x2, Pallas kernels, body(): pl.pallas_call(functools.partial(transform_kernel, tuple((g * GROUP for g...  36.1 us
    all_to_all x1, waiting for transfers between devices, body(): increment = lax.all_to_all(increment, 'band', 0, 0, tiled=True)  32.2 us
    pallas_call x4, Pallas kernels, body(): pl.pallas_call(table_kernel, out_shape=jax.ShapeDtypeStruct((2, half // 1...  20 us
    all_to_all x2, waiting for transfers between devices, body(): gathered = lax.all_to_all(synth, 'band', 0, 0, tiled=True)  15.8 us
    dot_general x2, matrix products, body(): lax.dot_general(forward[n].reshape(bands * rows[n], bands, lon), spread,...  11.5 us
    all_to_all x2, starting transfers between devices, body(): gathered = lax.all_to_all(synth, 'band', 0, 0, tiled=True)  10.9 us
  transfers between devices with their start and end apart: 9, of which 7 were waited for; matrix products, arithmetic and copies ran while one was open for 7% of the time, Pallas kernels for 32%

profile of v2, /device:TPU:15, one launch (start us, length us, event | category | flops | bytes accessed | tf_op | source)
XLA Modules:
  0.0 296.1 jit_solution(13991070646052572844)
XLA Ops:
  0.0 1.4 slice.55
  1.4 1.9 collective-permute-start.2
  3.3 0.9 slice_bitcast_fusion
  4.2 0.1 collective-permute-start.1
  4.3 0.8 slice.52
  5.0 0.8 slice.53
  5.8 1.7 collective-permute-start
  7.5 0.8 collective-permute-done.e_ref
  8.3 0.0 copy-start.5
  8.3 0.0 collective-permute-done.1.h_ref
  8.3 0.0 copy-start.4
  8.3 0.0 collective-permute-done.2.h_ref
  8.3 0.6 copy-done.5
  8.9 0.0 copy-done.4
  8.9 10.9 %advect_first.1 = (f32[6,128,1024]{2,1,0:T(8,128)}, f32[16,6,64,128]{3,2,1,0:T(8,128)}) custom-call(f32[7,6,128,1024]{3,2,1,0:T(8,128)} %s_ref.3, f32[6,2,1024]{2,1,0:T(2,128)} %copy-done.4, f32[2,1024]{1,0:T(2,128)} %copy-done.5, f32[128,1024]{1,0:T(8,128)} %lon_ref.3, f32[128,1024]{1,0:T(8,128)} %lat_ref.3, f32[6,128,1024]{2,1,0:T(8,128)} %f_ref.1), custom_call_target="tpu_custom_call" | custom-call | flops 11010048 | bytes 12582912 | tf_op jit(solution)/shard_map/advect_first/pallas_call | solution.py:258
  19.8 0.0 copy-done.3
  19.8 0.0 copy-start.6
  19.8 7.5 %all-to-all-start = ((f32[16,6,64,128]{3,2,1,0:T(8,128)}), f32[16,6,64,128]{3,2,1,0:T(8,128)S(1)}, u32[]{:S(2)}, u32[]{:S(2)}) async-start(f32[16,6,64,128]{3,2,1,0:T(8,128)} %get-tuple-element.18), calls=%async_computation | async-start | bytes 6291456 | tf_op jit(solution)/shard_map/all_to_all | solution.py:281
  27.3 0.7 multiply_bitcast_fusion
  28.0 0.1 slice_bitcast_fusion.1
  28.1 0.0 copy-done.6
  28.1 0.1 add_add_fusion
  28.1 0.6 fusion.10
  28.8 0.7 broadcast_in_dim.18.wave_ref
  29.4 2.8 legendre_table.7.refs_2_
  32.2 0.7 broadcast_in_dim.17.wave_ref
  32.9 4.2 %legendre_table.6.refs_2_ = f32[2,4,1024,128]{3,2,1,0:T(8,128)} custom-call(f32[8,512]{1,0:T(8,128)} %get-tuple-element.26.start_ref, f32[8,128]{1,0:T(8,128)} %broadcast_in_dim.17.wave_ref, f32[1,512]{1,0:T(1,128)} %constant.40.clone.mu_ref), custom_call_target="tpu_custom_call" | custom-call | flops 8388608 | bytes 4194304 | tf_op jit(solution)/shard_map/legendre_table/pallas_call | solution.py:339
  37.1 0.7 broadcast_in_dim.16.wave_ref
  37.8 5.7 %legendre_table.5.refs_1_ = f32[2,4,1536,128]{3,2,1,0:T(8,128)} custom-call(f32[8,512]{1,0:T(8,128)} %get-tuple-element.27.start_ref, f32[8,128]{1,0:T(8,128)} %broadcast_in_dim.16.wave_ref, f32[1,512]{1,0:T(1,128)} %constant.40.clone.mu_ref), custom_call_target="tpu_custom_call" | custom-call | flops 12582912 | bytes 6291456 | tf_op jit(solution)/shard_map/legendre_table/pallas_call | solution.py:339
  43.5 0.7 broadcast_in_dim.15.wave_ref
  44.2 7.2 %legendre_table.4.refs_1_ = f32[2,4,2048,128]{3,2,1,0:T(8,128)} custom-call(f32[8,512]{1,0:T(8,128)} %get-tuple-element.28.start_ref, f32[8,128]{1,0:T(8,128)} %broadcast_in_dim.15.wave_ref, f32[1,512]{1,0:T(1,128)} %constant.40.clone.mu_ref), custom_call_target="tpu_custom_call" | custom-call | flops 16777216 | bytes 8388608 | tf_op jit(solution)/shard_map/legendre_table/pallas_call | solution.py:339
  51.4 45.8 %all-to-all-done = f32[16,6,64,128]{3,2,1,0:T(8,128)S(1)} async-done(((f32[16,6,64,128]{3,2,1,0:T(8,128)}), f32[16,6,64,128]{3,2,1,0:T(8,128)S(1)}, u32[]{:S(2)}, u32[]{:S(2)}) %all-to-all-start) | async-done | bytes 3145760 | tf_op jit(solution)/shard_map/all_to_all | solution.py:281
  97.2 5.7 %fusion.4 = f32[512,6,64]{0,2,1:T(8,128)} fusion(f32[16,6,64,128]{3,2,1,0:T(8,128)S(1)} %all-to-all-done, f32[512,16,128,1]{2,0,1,3:T(8,128)} %constant.51), kind=kOutput, calls=%fused_computation.6 | convolution fusion | flops 2415919104 | bytes 8126464 | tf_op jit(solution)/shard_map/dot_general | solution.py:352
  102.9 3.1 %copy.22 = f32[512,6,64]{2,1,0:T(8,128)} copy(f32[512,6,64]{0,2,1:T(8,128)} %fusion.4) | data formatting | bytes 1572864 | tf_op jit(solution)/shard_map/dot_general | solution.py:352
  106.0 2.7 reshape.56
  108.6 4.9 %all-to-all-start.1 = ((f32[16,32,384]{2,1,0:T(8,128)}), f32[16,32,384]{2,1,0:T(8,128)}, u32[]{:S(2)}, u32[]{:S(2)}) async-start(f32[16,32,384]{2,1,0:T(8,128)} %reshape.56), calls=%async_computation.1 | async-start | bytes 1572864 | tf_op jit(solution)/shard_map/all_to_all | solution.py:359
  113.5 5.7 %fusion.7 = f32[512,6,64]{0,2,1:T(8,128)} fusion(f32[16,6,64,128]{3,2,1,0:T(8,128)S(1)} %all-to-all-done, f32[512,16,128,1]{2,0,1,3:T(8,128)} %constant.52), kind=kOutput, calls=%fused_computation.7 | convolution fusion | flops 2415919104 | bytes 8126464 | tf_op jit(solution)/shard_map/dot_general | solution.py:352
  119.3 0.0 copy-start.7
  119.3 1.9 copy.25
  121.2 1.4 reshape.60
  122.6 10.2 %all-to-all-done.1.refs_0_ = f32[16,32,384]{2,1,0:T(8,128)} async-done(((f32[16,32,384]{2,1,0:T(8,128)}), f32[16,32,384]{2,1,0:T(8,128)}, u32[]{:S(2)}, u32[]{:S(2)}) %all-to-all-start.1) | async-done | bytes 786464 | tf_op jit(solution)/shard_map/all_to_all | solution.py:359
  132.9 5.0 %all-to-all-start.3 = ((f32[16,32,384]{2,1,0:T(8,128)}), f32[16,32,384]{2,1,0:T(8,128)S(1)}, u32[]{:S(2)}, u32[]{:S(2)}) async-start(f32[16,32,384]{2,1,0:T(8,128)} %reshape.60), calls=%async_computation.3 | async-start | bytes 1572864 | tf_op jit(solution)/shard_map/all_to_all | solution.py:359
  137.8 0.0 copy-done.7
  137.8 0.1 pad_dynamic-slice_fusion
  137.9 0.2 reshape.57
  138.1 0.7 copy.23
  138.8 18.1 %legendre_transform.2 = f32[16,32,384]{2,1,0:T(8,128)} custom-call(f32[16,32,384]{2,1,0:T(8,128)} %all-to-all-done.1.refs_0_, f32[2,4,2048,128]{3,2,1,0:T(8,128)} %legendre_table.4.refs_1_, f32[2,4,512,128]{3,2,1,0:T(8,128)} %legendre_table.7.refs_2_, f32[2,512]{1,0:T(2,128)} %bitcast.53, f32[1,512]{1,0:T(1,128)} %constant.41.clone.refs_4_, ...), custom_call_target="tpu_custom_call" | custom-call | flops 786432000 | bytes 10485760 | tf_op jit(solution)/shard_map/legendre_transform/pallas_call | solution.py:361
  157.0 0.1 all-to-all-done.3.refs_0_
  157.1 0.0 copy-start.1
  157.1 5.9 %all-to-all-start.2 = ((f32[16,32,384]{2,1,0:T(8,128)}), f32[16,32,384]{2,1,0:T(8,128)S(1)}, u32[]{:S(2)}, u32[]{:S(2)}) async-start(f32[16,32,384]{2,1,0:T(8,128)} %legendre_transform.2), calls=%async_computation.2 | async-start | bytes 1572864 | tf_op jit(solution)/shard_map/all_to_all | solution.py:371
  163.0 0.0 copy-done.1
  163.0 18.0 %legendre_transform.3 = f32[16,32,384]{2,1,0:T(8,128)} custom-call(f32[16,32,384]{2,1,0:T(8,128)} %copy-done.1, f32[2,4,1536,128]{3,2,1,0:T(8,128)} %legendre_table.5.refs_1_, f32[2,4,1024,128]{3,2,1,0:T(8,128)} %legendre_table.6.refs_2_, f32[2,512]{1,0:T(2,128)} %bitcast.54, f32[1,512]{1,0:T(1,128)} %constant.41.clone.refs_4_, ...), custom_call_target="tpu_custom_call" | custom-call | flops 786432000 | bytes 10485760 | tf_op jit(solution)/shard_map/legendre_transform/pallas_call | solution.py:361
  181.0 1.3 all-to-all-done.2
  182.2 5.0 %all-to-all-start.4 = ((f32[16,32,384]{2,1,0:T(8,128)}), f32[16,32,384]{2,1,0:T(8,128)}, u32[]{:S(2)}, u32[]{:S(2)}) async-start(f32[16,32,384]{2,1,0:T(8,128)} %legendre_transform.3), calls=%async_computation.4 | async-start | bytes 1572864 | tf_op jit(solution)/shard_map/all_to_all | solution.py:371
  187.2 0.0 copy-done.2
  187.2 4.8 %fusion.11 = f32[384,2048]{1,0:T(8,128)S(1)} fusion(f32[512,384]{1,0:T(8,128)} %bitcast.52, f32[512,2048]{1,0:T(8,128)} %constant.37.clone), kind=kOutput, calls=%fused_computation.20 | convolution fusion | flops 2415919104 | bytes 8126464 | tf_op jit(solution)/shard_map/dot_general | solution.py:372
  192.0 14.5 %all-to-all-done.4 = f32[16,32,384]{2,1,0:T(8,128)} async-done(((f32[16,32,384]{2,1,0:T(8,128)}), f32[16,32,384]{2,1,0:T(8,128)}, u32[]{:S(2)}, u32[]{:S(2)}) %all-to-all-start.4) | async-done | bytes 786464 | tf_op jit(solution)/shard_map/all_to_all | solution.py:371
  206.5 4.8 %add_bitcast_fusion = f32[48,16,8,128]{3,2,1,0:T(8,128)S(1)} fusion(f32[384,2048]{1,0:T(8,128)S(1)} %fusion.11, f32[512,384]{1,0:T(8,128)} %bitcast.14, f32[512,2048]{1,0:T(8,128)} %constant.39.clone), kind=kOutput, calls=%fused_computation.5 | convolution fusion | flops 2416705536 | bytes 11272192 | tf_op jit(solution)/shard_map/dot_general | solution.py:372
  211.3 2.0 copy.31
  213.3 4.9 %all-to-all-start.5 = ((f32[16,6,64,128]{3,2,1,0:T(8,128)}), f32[16,6,64,128]{3,2,1,0:T(8,128)S(1)}, u32[]{:S(2)}, u32[]{:S(2)}) async-start(f32[16,6,64,128]{3,2,1,0:T(8,128)} %bitcast.51), calls=%async_computation.5 | async-start | bytes 6291456 | tf_op jit(solution)/shard_map/all_to_all | solution.py:380
  218.3 37.7 %advect_rest.1.b_ref = f32[7,6,128,1024]{3,2,1,0:T(8,128)} custom-call(f32[7,6,128,1024]{3,2,1,0:T(8,128)} %s_ref.3, f32[6,6,2,1024]{3,2,1,0:T(2,128)} %copy-done.3, f32[2,1024]{1,0:T(2,128)} %copy-done.5, f32[128,1024]{1,0:T(8,128)} %lon_ref.3, f32[128,1024]{1,0:T(8,128)} %lat_ref.3), custom_call_target="tpu_custom_call" | custom-call | flops 66060288 | bytes 37748736 | tf_op jit(solution)/shard_map/advect_rest/pallas_call | solution.py:284
  256.0 32.2 %all-to-all-done.5.t_ref = f32[16,6,64,128]{3,2,1,0:T(8,128)S(1)} async-done(((f32[16,6,64,128]{3,2,1,0:T(8,128)}), f32[16,6,64,128]{3,2,1,0:T(8,128)S(1)}, u32[]{:S(2)}, u32[]{:S(2)}) %all-to-all-start.5) | async-done | bytes 3145760 | tf_op jit(solution)/shard_map/all_to_all | solution.py:380
  288.2 1.7 copy-done
  289.8 6.3 %add_increment.1 = f32[7,6,128,1024]{3,2,1,0:T(8,128)} custom-call(f32[6,128,1024]{2,1,0:T(8,128)} %get-tuple-element.17.a_ref, f32[16,6,64,128]{3,2,1,0:T(8,128)} %copy-done, f32[7,6,128,1024]{3,2,1,0:T(8,128)} %advect_rest.1.b_ref), custom_call_target="tpu_custom_call", output_to_operand_aliasing={{}: (2, {})} | custom-call | flops 786432 | bytes 9437184 | tf_op jit(solution)/shard_map/add_increment/pallas_call | solution.py:382
  (6 shorter events, 0.0 us)
Async XLA Ops:
  1.4 6.9 %collective-permute-start.2 = (f32[6,6,2,1024]{3,2,1,0:T(2,128)S(1)}, f32[6,6,2,1024]{3,2,1,0:T(2,128)S(1)}, u32[]{:S(2)}, u32[]{:S(2)}) collective-permute-start(f32[6,6,2,1024]{3,2,1,0:T(2,128)S(1)} %slice.55), channel_id=1, source_target_pairs={{0,1},{1,2},{2,3},{3,4},{4,5},{5,6},{6,7},{7,8},{8,9},{9,10},{10,1... | collective-permute-start | bytes 884744 | tf_op jit(solution)/shard_map/ppermute | solution.py:21
  4.2 4.1 %collective-permute-start.1 = (f32[6,2,1024]{2,1,0:T(2,128)S(1)}, f32[6,2,1024]{2,1,0:T(2,128)S(1)}, u32[]{:S(2)}, u32[]{:S(2)}) collective-permute-start(f32[6,2,1024]{2,1,0:T(2,128)S(1)} %slice_bitcast_fusion), channel_id=1, source_target_pairs={{0,1},{1,2},{2,3},{3,4},{4,5},{5,6},{6,7},{7,8},{8,9},{9,10},{10,1... | collective-permute-start | bytes 147464 | tf_op jit(solution)/shard_map/ppermute | solution.py:21
  5.8 2.5 collective-permute-start
  8.3 0.6 copy-start.5
  8.3 0.6 copy-start.4
  8.9 10.9 %copy-start.3 = (f32[6,6,2,1024]{3,2,1,0:T(2,128)}, f32[6,6,2,1024]{3,2,1,0:T(2,128)S(1)}, u32[]{:S(2)}) copy-start(f32[6,6,2,1024]{3,2,1,0:T(2,128)S(1)} %collective-permute-done.2.h_ref) | copy-start | bytes 884740
  19.8 8.3 %copy-start.6 = (f32[512]{0:T(512)S(1)}, f32[512]{0:T(512)}, u32[]{:S(2)}) copy-start(f32[512]{0:T(512)} %constant.42.clone) | copy-start | bytes 6148
  19.8 77.4 %all-to-all-start = ((f32[16,6,64,128]{3,2,1,0:T(8,128)}), f32[16,6,64,128]{3,2,1,0:T(8,128)S(1)}, u32[]{:S(2)}, u32[]{:S(2)}) async-start(f32[16,6,64,128]{3,2,1,0:T(8,128)} %get-tuple-element.18), calls=%async_computation | async-start | bytes 6291456 | tf_op jit(solution)/shard_map/all_to_all | solution.py:281
  108.6 24.2 %all-to-all-start.1 = ((f32[16,32,384]{2,1,0:T(8,128)}), f32[16,32,384]{2,1,0:T(8,128)}, u32[]{:S(2)}, u32[]{:S(2)}) async-start(f32[16,32,384]{2,1,0:T(8,128)} %reshape.56), calls=%async_computation.1 | async-start | bytes 1572864 | tf_op jit(solution)/shard_map/all_to_all | solution.py:359
  119.3 18.6 %copy-start.7 = (f32[512]{0:T(512)S(1)}, f32[512]{0:T(512)}, u32[]{:S(2)}) copy-start(f32[512]{0:T(512)} %param.18) | copy-start | bytes 6148
  132.9 24.2 %all-to-all-start.3 = ((f32[16,32,384]{2,1,0:T(8,128)}), f32[16,32,384]{2,1,0:T(8,128)S(1)}, u32[]{:S(2)}, u32[]{:S(2)}) async-start(f32[16,32,384]{2,1,0:T(8,128)} %reshape.60), calls=%async_computation.3 | async-start | bytes 1572864 | tf_op jit(solution)/shard_map/all_to_all | solution.py:359
  157.1 5.9 %copy-start.1 = (f32[16,32,384]{2,1,0:T(8,128)}, f32[16,32,384]{2,1,0:T(8,128)S(1)}, u32[]{:S(2)}) copy-start(f32[16,32,384]{2,1,0:T(8,128)S(1)} %all-to-all-done.3.refs_0_) | copy-start | bytes 2359300
  157.1 25.2 %all-to-all-start.2 = ((f32[16,32,384]{2,1,0:T(8,128)}), f32[16,32,384]{2,1,0:T(8,128)S(1)}, u32[]{:S(2)}, u32[]{:S(2)}) async-start(f32[16,32,384]{2,1,0:T(8,128)} %legendre_transform.2), calls=%async_computation.2 | async-start | bytes 1572864 | tf_op jit(solution)/shard_map/all_to_all | solution.py:371
  182.2 5.0 %copy-start.2 = (f32[16,32,384]{2,1,0:T(8,128)}, f32[16,32,384]{2,1,0:T(8,128)S(1)}, u32[]{:S(2)}) copy-start(f32[16,32,384]{2,1,0:T(8,128)S(1)} %all-to-all-done.2) | copy-start | bytes 2359300
  182.2 24.3 %all-to-all-start.4 = ((f32[16,32,384]{2,1,0:T(8,128)}), f32[16,32,384]{2,1,0:T(8,128)}, u32[]{:S(2)}, u32[]{:S(2)}) async-start(f32[16,32,384]{2,1,0:T(8,128)} %legendre_transform.3), calls=%async_computation.4 | async-start | bytes 1572864 | tf_op jit(solution)/shard_map/all_to_all | solution.py:371
  213.3 74.8 %all-to-all-start.5 = ((f32[16,6,64,128]{3,2,1,0:T(8,128)}), f32[16,6,64,128]{3,2,1,0:T(8,128)S(1)}, u32[]{:S(2)}, u32[]{:S(2)}) async-start(f32[16,6,64,128]{3,2,1,0:T(8,128)} %bitcast.51), calls=%async_computation.5 | async-start | bytes 6291456 | tf_op jit(solution)/shard_map/all_to_all | solution.py:380
  288.2 1.7 copy-start

commit v3 on v2

--- a/solution.py
+++ b/solution.py
@@ -347,12 +347,14 @@
 
     spread, *tables = lax.optimization_barrier((spread, *tables))
     rows = [2 * GROUP * len(chunk) for chunk in chunks]
+    circles = spread.reshape(bands, levels * lat_local, lon).transpose(1, 0, 2)
+    circles = circles.reshape(levels * lat_local, lon_total)
     increment = 0.0
     for n, chunk in enumerate(chunks):
         fourier = lax.dot_general(
-            forward[n].reshape(bands * rows[n], bands, lon),
-            spread,
-            (((1, 2), (0, 3)), ((), ())),
+            forward[n],
+            circles,
+            (((1,), (1,)), ((), ())),
             precision=lax.Precision.HIGH,
         )
         fourier = fourier.reshape(bands, rows[n], levels * lat_local)

time: 298 us -> 296 us (level)
  local copies, waits for them, and re-layouts: 21.6 us -> 16.4 us
  waiting for transfers between devices: 105 us -> 108 us
    dot_general x2 -> x0, local copies, waits for them, and re-layouts: 4.99 us -> none  [body(): lax.dot_general(forward[n].reshape(bands * rows[n], bands, lon), spread,...]
  transfers between devices with their start and end apart: 9 -> 9, of which waited for: 7 -> 7; matrix products, arithmetic and copies ran while one was open for 7% -> 6% of each run, Pallas kernels for 32% -> 32%
where the time goes in v3:
time: 296 us; the launch traced here: 295 us
  Pallas kernels  111 us (38%)
  waiting for transfers between devices  108 us (36%)
  starting transfers between devices  36.6 us (12%)
  matrix products  22.6 us (8%)
  local copies, waits for them, and re-layouts  16.4 us (6%)
    all_to_all x1, waiting for transfers between devices, body(): spread = lax.all_to_all(turned, 'band', 0, 0, tiled=True)  45.7 us
    pallas_call x1, Pallas kernels, body(): pl.pallas_call(rest_kernel, grid=(fields - 1, levels // per), in_specs=[p...  37.7 us
    pallas_call x2, Pallas kernels, body(): pl.pallas_call(functools.partial(transform_kernel, tuple((g * GROUP for g...  36 us
    all_to_all x1, waiting for transfers between devices, body(): increment = lax.all_to_all(increment, 'band', 0, 0, tiled=True)  32.2 us
    pallas_call x4, Pallas kernels, body(): pl.pallas_call(table_kernel, out_shape=jax.ShapeDtypeStruct((2, half // 1...  20.1 us
    all_to_all x2, waiting for transfers between devices, body(): gathered = lax.all_to_all(synth, 'band', 0, 0, tiled=True)  15.8 us
    dot_general x2, matrix products, body(): lax.dot_general(forward[n], circles, (((1,), (1,)), ((), ())), precision=...  13.1 us
    all_to_all x2, waiting for transfers between devices, body(): owned = lax.all_to_all(fourier, 'band', 0, 0, tiled=True)  13 us
  transfers between devices with their start and end apart: 9, of which 7 were waited for; matrix products, arithmetic and copies ran while one was open for 6% of the time, Pallas kernels for 32%

profile of v3, /device:TPU:15, one launch (start us, length us, event | category | flops | bytes accessed | tf_op | source)
XLA Modules:
  0.0 295.0 jit_solution(536037345277636356)
XLA Ops:
  0.0 1.4 slice.55
  1.4 1.9 collective-permute-start.2
  3.3 0.9 slice_bitcast_fusion
  4.2 0.1 collective-permute-start.1
  4.3 0.8 slice.52
  5.0 0.8 slice.53
  5.8 1.7 collective-permute-start
  7.5 0.8 collective-permute-done.e_ref
  8.3 0.0 copy-start.6
  8.3 0.0 collective-permute-done.1.h_ref
  8.3 0.0 copy-start.5
  8.3 0.0 collective-permute-done.2.h_ref
  8.3 0.6 copy-done.6
  8.9 0.0 copy-done.5
  8.9 10.9 %advect_first.1 = (f32[6,128,1024]{2,1,0:T(8,128)}, f32[16,6,64,128]{3,2,1,0:T(8,128)}) custom-call(f32[7,6,128,1024]{3,2,1,0:T(8,128)} %s_ref.3, f32[6,2,1024]{2,1,0:T(2,128)} %copy-done.5, f32[2,1024]{1,0:T(2,128)} %copy-done.6, f32[128,1024]{1,0:T(8,128)} %lon_ref.3, f32[128,1024]{1,0:T(8,128)} %lat_ref.3, f32[6,128,1024]{2,1,0:T(8,128)} %f_ref.1), custom_call_target="tpu_custom_call" | custom-call | flops 11010048 | bytes 12582912 | tf_op jit(solution)/shard_map/advect_first/pallas_call | solution.py:258
  19.8 0.0 copy-done.4
  19.8 0.0 copy-start.7
  19.8 7.5 %all-to-all-start = ((f32[16,6,64,128]{3,2,1,0:T(8,128)}), f32[16,6,64,128]{3,2,1,0:T(8,128)S(1)}, u32[]{:S(2)}, u32[]{:S(2)}) async-start(f32[16,6,64,128]{3,2,1,0:T(8,128)} %get-tuple-element.18), calls=%async_computation | async-start | bytes 6291456 | tf_op jit(solution)/shard_map/all_to_all | solution.py:281
  27.3 0.7 multiply_bitcast_fusion
  28.0 0.1 slice_bitcast_fusion.1
  28.0 0.0 copy-done.7
  28.0 0.1 add_add_fusion
  28.1 0.6 fusion
  28.7 0.7 broadcast_in_dim.18.wave_ref
  29.4 2.8 legendre_table.7.refs_2_
  32.2 0.7 broadcast_in_dim.17.wave_ref
  32.9 4.3 %legendre_table.6.refs_2_ = f32[2,4,1024,128]{3,2,1,0:T(8,128)} custom-call(f32[8,512]{1,0:T(8,128)} %get-tuple-element.26.start_ref, f32[8,128]{1,0:T(8,128)} %broadcast_in_dim.17.wave_ref, f32[1,512]{1,0:T(1,128)} %constant.40.clone.mu_ref), custom_call_target="tpu_custom_call" | custom-call | flops 8388608 | bytes 4194304 | tf_op jit(solution)/shard_map/legendre_table/pallas_call | solution.py:339
  37.2 0.7 broadcast_in_dim.16.wave_ref
  37.9 5.7 %legendre_table.5.refs_1_ = f32[2,4,1536,128]{3,2,1,0:T(8,128)} custom-call(f32[8,512]{1,0:T(8,128)} %get-tuple-element.27.start_ref, f32[8,128]{1,0:T(8,128)} %broadcast_in_dim.16.wave_ref, f32[1,512]{1,0:T(1,128)} %constant.40.clone.mu_ref), custom_call_target="tpu_custom_call" | custom-call | flops 12582912 | bytes 6291456 | tf_op jit(solution)/shard_map/legendre_table/pallas_call | solution.py:339
  43.6 0.7 broadcast_in_dim.15.wave_ref
  44.2 7.2 %legendre_table.4.refs_1_ = f32[2,4,2048,128]{3,2,1,0:T(8,128)} custom-call(f32[8,512]{1,0:T(8,128)} %get-tuple-element.28.start_ref, f32[8,128]{1,0:T(8,128)} %broadcast_in_dim.15.wave_ref, f32[1,512]{1,0:T(1,128)} %constant.40.clone.mu_ref), custom_call_target="tpu_custom_call" | custom-call | flops 16777216 | bytes 8388608 | tf_op jit(solution)/shard_map/legendre_table/pallas_call | solution.py:339
  51.4 45.7 %all-to-all-done = f32[16,6,64,128]{3,2,1,0:T(8,128)S(1)} async-done(((f32[16,6,64,128]{3,2,1,0:T(8,128)}), f32[16,6,64,128]{3,2,1,0:T(8,128)S(1)}, u32[]{:S(2)}, u32[]{:S(2)}) %all-to-all-start) | async-done | bytes 3145760 | tf_op jit(solution)/shard_map/all_to_all | solution.py:281
  97.2 0.0 copy-start.1
  97.2 1.6 copy-done.1
  98.8 2.4 copy.17
  101.2 6.5 %fusion.1 = f32[512,384]{1,0:T(8,128)} fusion(f32[512,2048]{1,0:T(8,128)} %constant.36.clone, f32[384,2048]{0,1:T(8,128)S(1)} %bitcast.37), kind=kOutput, calls=%fused_computation.14 | convolution fusion | flops 2415919104 | bytes 8126464 | tf_op jit(solution)/shard_map/dot_general | solution.py:354
  107.7 4.9 %all-to-all-start.1 = ((f32[16,32,384]{2,1,0:T(8,128)}), f32[16,32,384]{2,1,0:T(8,128)}, u32[]{:S(2)}, u32[]{:S(2)}) async-start(f32[16,32,384]{2,1,0:T(8,128)} %bitcast.43), calls=%async_computation.1 | async-start | bytes 1572864 | tf_op jit(solution)/shard_map/all_to_all | solution.py:361
  112.6 0.0 copy-start.8
  112.6 6.6 %fusion.3 = f32[512,384]{1,0:T(8,128)} fusion(f32[512,2048]{1,0:T(8,128)} %constant.38.clone, f32[384,2048]{0,1:T(8,128)S(1)} %bitcast.38), kind=kOutput, calls=%fused_computation.16 | convolution fusion | flops 2415919104 | bytes 8126464 | tf_op jit(solution)/shard_map/dot_general | solution.py:354
  119.1 12.8 %all-to-all-done.1.refs_0_ = f32[16,32,384]{2,1,0:T(8,128)} async-done(((f32[16,32,384]{2,1,0:T(8,128)}), f32[16,32,384]{2,1,0:T(8,128)}, u32[]{:S(2)}, u32[]{:S(2)}) %all-to-all-start.1) | async-done | bytes 786464 | tf_op jit(solution)/shard_map/all_to_all | solution.py:361
  131.9 5.0 %all-to-all-start.3 = ((f32[16,32,384]{2,1,0:T(8,128)}), f32[16,32,384]{2,1,0:T(8,128)S(1)}, u32[]{:S(2)}, u32[]{:S(2)}) async-start(f32[16,32,384]{2,1,0:T(8,128)} %bitcast.41), calls=%async_computation.3 | async-start | bytes 1572864 | tf_op jit(solution)/shard_map/all_to_all | solution.py:361
  136.9 0.0 copy-done.8
  136.9 0.1 pad_dynamic-slice_fusion
  137.0 0.2 reshape.58
  137.2 0.7 copy.18
  137.9 18.0 %legendre_transform.2 = f32[16,32,384]{2,1,0:T(8,128)} custom-call(f32[16,32,384]{2,1,0:T(8,128)} %all-to-all-done.1.refs_0_, f32[2,4,2048,128]{3,2,1,0:T(8,128)} %legendre_table.4.refs_1_, f32[2,4,512,128]{3,2,1,0:T(8,128)} %legendre_table.7.refs_2_, f32[2,512]{1,0:T(2,128)} %bitcast.44, f32[1,512]{1,0:T(1,128)} %constant.41.clone.refs_4_, ...), custom_call_target="tpu_custom_call" | custom-call | flops 786432000 | bytes 10485760 | tf_op jit(solution)/shard_map/legendre_transform/pallas_call | solution.py:363
  155.9 0.2 all-to-all-done.3.refs_0_
  156.1 0.0 copy-start.2
  156.1 5.8 %all-to-all-start.2 = ((f32[16,32,384]{2,1,0:T(8,128)}), f32[16,32,384]{2,1,0:T(8,128)S(1)}, u32[]{:S(2)}, u32[]{:S(2)}) async-start(f32[16,32,384]{2,1,0:T(8,128)} %legendre_transform.2), calls=%async_computation.2 | async-start | bytes 1572864 | tf_op jit(solution)/shard_map/all_to_all | solution.py:373
  161.9 0.0 copy-done.2
  161.9 18.0 %legendre_transform.3 = f32[16,32,384]{2,1,0:T(8,128)} custom-call(f32[16,32,384]{2,1,0:T(8,128)} %copy-done.2, f32[2,4,1536,128]{3,2,1,0:T(8,128)} %legendre_table.5.refs_1_, f32[2,4,1024,128]{3,2,1,0:T(8,128)} %legendre_table.6.refs_2_, f32[2,512]{1,0:T(2,128)} %bitcast.45, f32[1,512]{1,0:T(1,128)} %constant.41.clone.refs_4_, ...), custom_call_target="tpu_custom_call" | custom-call | flops 786432000 | bytes 10485760 | tf_op jit(solution)/shard_map/legendre_transform/pallas_call | solution.py:363
  179.9 1.3 all-to-all-done.2
  181.2 0.0 copy-start.3
  181.2 5.0 %all-to-all-start.4 = ((f32[16,32,384]{2,1,0:T(8,128)}), f32[16,32,384]{2,1,0:T(8,128)}, u32[]{:S(2)}, u32[]{:S(2)}) async-start(f32[16,32,384]{2,1,0:T(8,128)} %legendre_transform.3), calls=%async_computation.4 | async-start | bytes 1572864 | tf_op jit(solution)/shard_map/all_to_all | solution.py:373
  186.1 0.0 copy-done.3
  186.1 4.8 %fusion.2 = f32[384,2048]{1,0:T(8,128)S(1)} fusion(f32[512,384]{1,0:T(8,128)} %bitcast.42, f32[512,2048]{1,0:T(8,128)} %constant.37.clone), kind=kOutput, calls=%fused_computation.15 | convolution fusion | flops 2415919104 | bytes 8126464 | tf_op jit(solution)/shard_map/dot_general | solution.py:374
  190.9 14.5 %all-to-all-done.4 = f32[16,32,384]{2,1,0:T(8,128)} async-done(((f32[16,32,384]{2,1,0:T(8,128)}), f32[16,32,384]{2,1,0:T(8,128)}, u32[]{:S(2)}, u32[]{:S(2)}) %all-to-all-start.4) | async-done | bytes 786464 | tf_op jit(solution)/shard_map/all_to_all | solution.py:373
  205.5 4.8 %add_bitcast_fusion = f32[48,16,8,128]{3,2,1,0:T(8,128)S(1)} fusion(f32[384,2048]{1,0:T(8,128)S(1)} %fusion.2, f32[512,384]{1,0:T(8,128)} %bitcast.14, f32[512,2048]{1,0:T(8,128)} %constant.39.clone), kind=kOutput, calls=%fused_computation.1 | convolution fusion | flops 2416705536 | bytes 11272192 | tf_op jit(solution)/shard_map/dot_general | solution.py:374
  210.3 1.9 copy.22
  212.2 5.0 %all-to-all-start.5 = ((f32[16,6,64,128]{3,2,1,0:T(8,128)}), f32[16,6,64,128]{3,2,1,0:T(8,128)S(1)}, u32[]{:S(2)}, u32[]{:S(2)}) async-start(f32[16,6,64,128]{3,2,1,0:T(8,128)} %bitcast.40), calls=%async_computation.5 | async-start | bytes 6291456 | tf_op jit(solution)/shard_map/all_to_all | solution.py:382
  217.2 37.7 %advect_rest.1.b_ref = f32[7,6,128,1024]{3,2,1,0:T(8,128)} custom-call(f32[7,6,128,1024]{3,2,1,0:T(8,128)} %s_ref.3, f32[6,6,2,1024]{3,2,1,0:T(2,128)} %copy-done.4, f32[2,1024]{1,0:T(2,128)} %copy-done.6, f32[128,1024]{1,0:T(8,128)} %lon_ref.3, f32[128,1024]{1,0:T(8,128)} %lat_ref.3), custom_call_target="tpu_custom_call" | custom-call | flops 66060288 | bytes 37748736 | tf_op jit(solution)/shard_map/advect_rest/pallas_call | solution.py:284
  254.8 32.2 %all-to-all-done.5.t_ref = f32[16,6,64,128]{3,2,1,0:T(8,128)S(1)} async-done(((f32[16,6,64,128]{3,2,1,0:T(8,128)}), f32[16,6,64,128]{3,2,1,0:T(8,128)S(1)}, u32[]{:S(2)}, u32[]{:S(2)}) %all-to-all-start.5) | async-done | bytes 3145760 | tf_op jit(solution)/shard_map/all_to_all | solution.py:382
  287.0 1.6 copy-done
  288.7 6.3 %add_increment.1 = f32[7,6,128,1024]{3,2,1,0:T(8,128)} custom-call(f32[6,128,1024]{2,1,0:T(8,128)} %get-tuple-element.17.a_ref, f32[16,6,64,128]{3,2,1,0:T(8,128)} %copy-done, f32[7,6,128,1024]{3,2,1,0:T(8,128)} %advect_rest.1.b_ref), custom_call_target="tpu_custom_call", output_to_operand_aliasing={{}: (2, {})} | custom-call | flops 786432 | bytes 9437184 | tf_op jit(solution)/shard_map/add_increment/pallas_call | solution.py:384
  (5 shorter events, 0.0 us)
Async XLA Ops:
  1.4 6.9 %collective-permute-start.2 = (f32[6,6,2,1024]{3,2,1,0:T(2,128)S(1)}, f32[6,6,2,1024]{3,2,1,0:T(2,128)S(1)}, u32[]{:S(2)}, u32[]{:S(2)}) collective-permute-start(f32[6,6,2,1024]{3,2,1,0:T(2,128)S(1)} %slice.55), channel_id=1, source_target_pairs={{0,1},{1,2},{2,3},{3,4},{4,5},{5,6},{6,7},{7,8},{8,9},{9,10},{10,1... | collective-permute-start | bytes 884744 | tf_op jit(solution)/shard_map/ppermute | solution.py:21
  4.2 4.1 %collective-permute-start.1 = (f32[6,2,1024]{2,1,0:T(2,128)S(1)}, f32[6,2,1024]{2,1,0:T(2,128)S(1)}, u32[]{:S(2)}, u32[]{:S(2)}) collective-permute-start(f32[6,2,1024]{2,1,0:T(2,128)S(1)} %slice_bitcast_fusion), channel_id=1, source_target_pairs={{0,1},{1,2},{2,3},{3,4},{4,5},{5,6},{6,7},{7,8},{8,9},{9,10},{10,1... | collective-permute-start | bytes 147464 | tf_op jit(solution)/shard_map/ppermute | solution.py:21
  5.8 2.5 collective-permute-start
  8.3 0.6 copy-start.6
  8.3 0.6 copy-start.5
  8.9 10.9 %copy-start.4 = (f32[6,6,2,1024]{3,2,1,0:T(2,128)}, f32[6,6,2,1024]{3,2,1,0:T(2,128)S(1)}, u32[]{:S(2)}) copy-start(f32[6,6,2,1024]{3,2,1,0:T(2,128)S(1)} %collective-permute-done.2.h_ref) | copy-start | bytes 884740
  19.8 8.3 %copy-start.7 = (f32[512]{0:T(512)S(1)}, f32[512]{0:T(512)}, u32[]{:S(2)}) copy-start(f32[512]{0:T(512)} %constant.42.clone) | copy-start | bytes 6148
  19.8 77.4 %all-to-all-start = ((f32[16,6,64,128]{3,2,1,0:T(8,128)}), f32[16,6,64,128]{3,2,1,0:T(8,128)S(1)}, u32[]{:S(2)}, u32[]{:S(2)}) async-start(f32[16,6,64,128]{3,2,1,0:T(8,128)} %get-tuple-element.18), calls=%async_computation | async-start | bytes 6291456 | tf_op jit(solution)/shard_map/all_to_all | solution.py:281
  97.2 1.6 copy-start.1
  107.7 24.2 %all-to-all-start.1 = ((f32[16,32,384]{2,1,0:T(8,128)}), f32[16,32,384]{2,1,0:T(8,128)}, u32[]{:S(2)}, u32[]{:S(2)}) async-start(f32[16,32,384]{2,1,0:T(8,128)} %bitcast.43), calls=%async_computation.1 | async-start | bytes 1572864 | tf_op jit(solution)/shard_map/all_to_all | solution.py:361
  112.6 24.3 %copy-start.8 = (f32[512]{0:T(512)S(1)}, f32[512]{0:T(512)}, u32[]{:S(2)}) copy-start(f32[512]{0:T(512)} %param.18) | copy-start | bytes 6148
  131.9 24.2 %all-to-all-start.3 = ((f32[16,32,384]{2,1,0:T(8,128)}), f32[16,32,384]{2,1,0:T(8,128)S(1)}, u32[]{:S(2)}, u32[]{:S(2)}) async-start(f32[16,32,384]{2,1,0:T(8,128)} %bitcast.41), calls=%async_computation.3 | async-start | bytes 1572864 | tf_op jit(solution)/shard_map/all_to_all | solution.py:361
  156.1 5.8 %copy-start.2 = (f32[16,32,384]{2,1,0:T(8,128)}, f32[16,32,384]{2,1,0:T(8,128)S(1)}, u32[]{:S(2)}) copy-start(f32[16,32,384]{2,1,0:T(8,128)S(1)} %all-to-all-done.3.refs_0_) | copy-start | bytes 2359300
  156.1 25.1 %all-to-all-start.2 = ((f32[16,32,384]{2,1,0:T(8,128)}), f32[16,32,384]{2,1,0:T(8,128)S(1)}, u32[]{:S(2)}, u32[]{:S(2)}) async-start(f32[16,32,384]{2,1,0:T(8,128)} %legendre_transform.2), calls=%async_computation.2 | async-start | bytes 1572864 | tf_op jit(solution)/shard_map/all_to_all | solution.py:373
  181.2 5.0 %copy-start.3 = (f32[16,32,384]{2,1,0:T(8,128)}, f32[16,32,384]{2,1,0:T(8,128)S(1)}, u32[]{:S(2)}) copy-start(f32[16,32,384]{2,1,0:T(8,128)S(1)} %all-to-all-done.2) | copy-start | bytes 2359300
  181.2 24.3 %all-to-all-start.4 = ((f32[16,32,384]{2,1,0:T(8,128)}), f32[16,32,384]{2,1,0:T(8,128)}, u32[]{:S(2)}, u32[]{:S(2)}) async-start(f32[16,32,384]{2,1,0:T(8,128)} %legendre_transform.3), calls=%async_computation.4 | async-start | bytes 1572864 | tf_op jit(solution)/shard_map/all_to_all | solution.py:373
  212.2 74.8 %all-to-all-start.5 = ((f32[16,6,64,128]{3,2,1,0:T(8,128)}), f32[16,6,64,128]{3,2,1,0:T(8,128)S(1)}, u32[]{:S(2)}, u32[]{:S(2)}) async-start(f32[16,6,64,128]{3,2,1,0:T(8,128)} %bitcast.40), calls=%async_computation.5 | async-start | bytes 6291456 | tf_op jit(solution)/shard_map/all_to_all | solution.py:382
  287.0 1.6 copy-start
